TPU v7x, 32 devices: a whole 2x2x4 slice. The times are simulated.
32 devices in a mesh: dp: 16 (over z, y, x), outer: 2 (over core).
Axes of the slice: x: 2, y: 2, z: 4, core: 2. Of those that a mesh axis runs over, the one named last changes fastest.
Arguments:
- patches: bfloat16 [384, 196, 768], P(('dp', 'outer'))
- image_counts: int32 [32], P(('dp', 'outer')), may hold values from 1 to 12, 288 in all
- grad_out: bfloat16 [384, 196, 768], P(('dp', 'outer')), may hold values from -6 to 6
- ln1_gain: bfloat16 [768], P('dp'), may hold values from 0.25 to 1.75
- ln1_bias: bfloat16 [768], P('dp'), may hold values from -1.5 to 1.5
- w_token_in: bfloat16 [196, 384], P(None, 'dp'), may hold values from -0.4375 to 0.4375
- b_token_in: bfloat16 [384], P('dp'), may hold values from -1.5 to 1.5
- w_token_out: bfloat16 [384, 196], P('dp'), may hold values from -0.625 to 0.625
- b_token_out: bfloat16 [196], replicated, may hold values from -1.5 to 1.5
- ln2_gain: bfloat16 [768], P('dp'), may hold values from 0.25 to 1.75
- ln2_bias: bfloat16 [768], P('dp'), may hold values from -1.5 to 1.5
- w_chan_in: bfloat16 [768, 3072], P('dp'), may hold values from -0.21875 to 0.21875
- b_chan_in: bfloat16 [3072], P('dp'), may hold values from -1.5 to 1.5
- w_chan_out: bfloat16 [3072, 768], P(None, 'dp'), may hold values from -0.21875 to 0.21875
- b_chan_out: bfloat16 [768], P('dp'), may hold values from -1.5 to 1.5
Outputs:
- mixed: bfloat16 [384, 196, 768], P(('dp', 'outer'))
- grad_patches: float32 [384, 196, 768], P(('dp', 'outer'))
- grad_ln1_gain: float32 [768], P('dp')
- grad_ln1_bias: float32 [768], P('dp')
- grad_w_token_in: float32 [196, 384], P(None, 'dp')
- grad_b_token_in: float32 [384], P('dp')
- grad_w_token_out: float32 [384, 196], P('dp')
- grad_b_token_out: float32 [196], replicated
- grad_ln2_gain: float32 [768], P('dp')
- grad_ln2_bias: float32 [768], P('dp')
- grad_w_chan_in: float32 [768, 3072], P('dp')
- grad_b_chan_in: float32 [3072], P('dp')
- grad_w_chan_out: float32 [3072, 768], P(None, 'dp')
- grad_b_chan_out: float32 [768], P('dp')
Inputs may be any that keep to these rules, and one draw needn't show every extreme that they name: `image_counts`: entry j counts the live images of device j along dp+outer; they are that device's first slots of its 12, the others are padding. Some device is full in every draw.
All inputs are finite; a program needn't handle non-finite values.
Results may differ from a plain program's by a relative error of at most 0.015.
Values may be sent and summed in bfloat16 or wider, within the bound.
A program may use at most 256 MiB of HBM per device.

v0:
```python
import jax
import jax.numpy as jnp
from jax import lax
from jax.sharding import PartitionSpec as P

eps = 1e-06


def normalize(values, gain, shift):
    average = jnp.mean(values, axis=-1, keepdims=True)
    centered = values - average
    variance = jnp.mean(centered * centered, axis=-1, keepdims=True)
    return centered * lax.rsqrt(variance + eps) * gain + shift


def gelu_back(pre_values, incoming):
    result, pull_back = jax.vjp(lambda values: jax.nn.gelu(values, approximate=True), pre_values)
    return pull_back(incoming)[0]


def activations(inputs, token_full, chan_full, tok_bout):
    gain_one, shift_one, tok_win, tok_bin, tok_wout = token_full
    gain_two, shift_two, chan_win, chan_bin, chan_wout, chan_bout = chan_full
    token_in = normalize(
        inputs, gain_one.astype(jnp.float32), shift_one.astype(jnp.float32)
    ).astype(jnp.bfloat16)
    token_pre = jnp.einsum(
        "isd,sk->idk", token_in, tok_win, preferred_element_type=jnp.float32
    ) + tok_bin.astype(jnp.float32)
    token_act = jax.nn.gelu(token_pre, approximate=True).astype(jnp.bfloat16)
    token_out = (
        jnp.einsum("idk,ks->isd", token_act, tok_wout, preferred_element_type=jnp.float32)
        + tok_bout.astype(jnp.float32)[:, None]
    )
    residual = inputs + token_out
    chan_in = normalize(
        residual, gain_two.astype(jnp.float32), shift_two.astype(jnp.float32)
    ).astype(jnp.bfloat16)
    chan_pre = jnp.einsum(
        "isd,dk->isk", chan_in, chan_win, preferred_element_type=jnp.float32
    ) + chan_bin.astype(jnp.float32)
    chan_act = jax.nn.gelu(chan_pre, approximate=True).astype(jnp.bfloat16)
    return (token_in, token_pre, token_act, residual, chan_in, chan_pre, chan_act)


def own_slice(vector, length):
    return lax.dynamic_slice_in_dim(vector, lax.axis_index("dp") * length, length)


def on_device(
    patches,
    image_counts,
    grad_out,
    ln1_gain,
    ln1_bias,
    w_token_in,
    b_token_in,
    w_token_out,
    b_token_out,
    ln2_gain,
    ln2_bias,
    w_chan_in,
    b_chan_in,
    w_chan_out,
    b_chan_out,
):
    slot_ids = jnp.arange(patches.shape[0], dtype=jnp.int32)
    keep_mask = (slot_ids < image_counts[0]).astype(jnp.float32)[:, None, None]
    token_full = (
        lax.all_gather(ln1_gain, "dp", axis=0, tiled=True),
        lax.all_gather(ln1_bias, "dp", axis=0, tiled=True),
        lax.all_gather(w_token_in, "dp", axis=1, tiled=True),
        lax.all_gather(b_token_in, "dp", axis=0, tiled=True),
        lax.all_gather(w_token_out, "dp", axis=0, tiled=True),
    )
    chan_full = (
        lax.all_gather(ln2_gain, "dp", axis=0, tiled=True),
        lax.all_gather(ln2_bias, "dp", axis=0, tiled=True),
        lax.all_gather(w_chan_in, "dp", axis=0, tiled=True),
        lax.all_gather(b_chan_in, "dp", axis=0, tiled=True),
        lax.all_gather(w_chan_out, "dp", axis=1, tiled=True),
        lax.all_gather(b_chan_out, "dp", axis=0, tiled=True),
    )
    inputs = patches.astype(jnp.float32)
    kept = activations(inputs, token_full, chan_full, b_token_out)
    chan_out = jnp.einsum(
        "isk,kd->isd", kept[6], chan_full[4], preferred_element_type=jnp.float32
    ) + chan_full[5].astype(jnp.float32)
    mixed = (keep_mask * (kept[3] + chan_out)).astype(jnp.bfloat16)
    token_full = (
        lax.all_gather(ln1_gain, "dp", axis=0, tiled=True),
        lax.all_gather(ln1_bias, "dp", axis=0, tiled=True),
        lax.all_gather(w_token_in, "dp", axis=1, tiled=True),
        lax.all_gather(b_token_in, "dp", axis=0, tiled=True),
        lax.all_gather(w_token_out, "dp", axis=0, tiled=True),
    )
    chan_full = (
        lax.all_gather(ln2_gain, "dp", axis=0, tiled=True),
        lax.all_gather(ln2_bias, "dp", axis=0, tiled=True),
        lax.all_gather(w_chan_in, "dp", axis=0, tiled=True),
        lax.all_gather(b_chan_in, "dp", axis=0, tiled=True),
        lax.all_gather(w_chan_out, "dp", axis=1, tiled=True),
        lax.all_gather(b_chan_out, "dp", axis=0, tiled=True),
    )
    kept = activations(inputs, token_full, chan_full, b_token_out)
    token_in, token_pre, token_act, residual, chan_in, chan_pre, chan_act = kept
    gain_one, shift_one, tok_win, tok_bin, tok_wout = token_full
    gain_two, shift_two, chan_win, chan_bin, chan_wout, chan_bout = chan_full
    masked_grad = keep_mask * grad_out.astype(jnp.float32)
    d_chan_out = masked_grad.astype(jnp.bfloat16)
    grad_chan_wout = jnp.einsum(
        "isk,isd->kd", chan_act, d_chan_out, preferred_element_type=jnp.float32
    )
    grad_chan_bout = jnp.sum(masked_grad, axis=(0, 1))
    d_chan_act = jnp.einsum(
        "isd,kd->isk", d_chan_out, chan_wout, preferred_element_type=jnp.float32
    )
    d_chan_pre = gelu_back(chan_pre, d_chan_act).astype(jnp.bfloat16)
    grad_chan_win = jnp.einsum(
        "isd,isk->dk", chan_in, d_chan_pre, preferred_element_type=jnp.float32
    )
    grad_chan_bin = jnp.sum(d_chan_pre.astype(jnp.float32), axis=(0, 1))
    d_chan_in = jnp.einsum("isk,dk->isd", d_chan_pre, chan_win, preferred_element_type=jnp.float32)
    normed, pull_two = jax.vjp(
        normalize, residual, gain_two.astype(jnp.float32), shift_two.astype(jnp.float32)
    )
    d_resid_norm, grad_gain_two, grad_shift_two = pull_two(d_chan_in)
    d_residual = masked_grad + d_resid_norm
    d_token_out = d_residual.astype(jnp.bfloat16)
    grad_tok_wout = jnp.einsum(
        "idk,isd->ks", token_act, d_token_out, preferred_element_type=jnp.float32
    )
    grad_tok_bout = jnp.sum(d_token_out.astype(jnp.float32), axis=(0, 2))
    d_token_act = jnp.einsum(
        "isd,ks->idk", d_token_out, tok_wout, preferred_element_type=jnp.float32
    )
    d_token_pre = gelu_back(token_pre, d_token_act).astype(jnp.bfloat16)
    grad_tok_win = jnp.einsum(
        "isd,idk->sk", token_in, d_token_pre, preferred_element_type=jnp.float32
    )
    grad_tok_bin = jnp.sum(d_token_pre.astype(jnp.float32), axis=(0, 1))
    d_token_in = jnp.einsum("idk,sk->isd", d_token_pre, tok_win, preferred_element_type=jnp.float32)
    normed_one, pull_one = jax.vjp(
        normalize, inputs, gain_one.astype(jnp.float32), shift_one.astype(jnp.float32)
    )
    d_input_norm, grad_gain_one, grad_shift_one = pull_one(d_token_in)
    grad_patches = d_residual + d_input_norm
    halves = (
        lax.psum_scatter(
            grad_tok_win.astype(jnp.bfloat16), "outer", scatter_dimension=0, tiled=True
        ).astype(jnp.float32),
        lax.psum_scatter(
            grad_tok_wout.astype(jnp.bfloat16), "outer", scatter_dimension=1, tiled=True
        ).astype(jnp.float32),
        lax.psum_scatter(
            grad_chan_win.astype(jnp.bfloat16), "outer", scatter_dimension=1, tiled=True
        ).astype(jnp.float32),
        lax.psum_scatter(
            grad_chan_wout.astype(jnp.bfloat16), "outer", scatter_dimension=0, tiled=True
        ).astype(jnp.float32),
    )
    owned = (
        lax.psum_scatter(halves[0], "dp", scatter_dimension=1, tiled=True),
        lax.psum_scatter(halves[1], "dp", scatter_dimension=0, tiled=True),
        lax.psum_scatter(halves[2], "dp", scatter_dimension=0, tiled=True),
        lax.psum_scatter(halves[3], "dp", scatter_dimension=1, tiled=True),
    )
    whole_owned = (
        lax.all_gather(owned[0].astype(jnp.bfloat16), "outer", axis=0, tiled=True).astype(
            jnp.float32
        ),
        lax.all_gather(owned[1].astype(jnp.bfloat16), "outer", axis=1, tiled=True).astype(
            jnp.float32
        ),
        lax.all_gather(owned[2].astype(jnp.bfloat16), "outer", axis=1, tiled=True).astype(
            jnp.float32
        ),
        lax.all_gather(owned[3].astype(jnp.bfloat16), "outer", axis=0, tiled=True).astype(
            jnp.float32
        ),
    )
    vectors = lax.psum(
        (
            grad_gain_one,
            grad_shift_one,
            grad_tok_bin,
            grad_gain_two,
            grad_shift_two,
            grad_chan_bin,
            grad_chan_bout,
            grad_tok_bout,
        ),
        ("dp", "outer"),
    )
    chan_width = ln1_gain.shape[0]
    token_width = b_token_in.shape[0]
    hidden_width = b_chan_in.shape[0]
    token_grads = (
        own_slice(vectors[0], chan_width),
        own_slice(vectors[1], chan_width),
        whole_owned[0],
        own_slice(vectors[2], token_width),
        whole_owned[1],
    )
    chan_grads = (
        own_slice(vectors[3], chan_width),
        own_slice(vectors[4], chan_width),
        whole_owned[2],
        own_slice(vectors[5], hidden_width),
        whole_owned[3],
        own_slice(vectors[6], chan_width),
    )
    shared_grad = vectors[7]
    return (
        mixed,
        grad_patches,
        token_grads[0],
        token_grads[1],
        token_grads[2],
        token_grads[3],
        token_grads[4],
        shared_grad,
        chan_grads[0],
        chan_grads[1],
        chan_grads[2],
        chan_grads[3],
        chan_grads[4],
        chan_grads[5],
    )


def solution(mesh):
    return jax.shard_map(
        on_device,
        mesh=mesh,
        in_specs=(
            P(("dp", "outer"), None, None),
            P(("dp", "outer")),
            P(("dp", "outer"), None, None),
            P("dp"),
            P("dp"),
            P(None, "dp"),
            P("dp"),
            P("dp", None),
            P(),
            P("dp"),
            P("dp"),
            P("dp", None),
            P("dp"),
            P(None, "dp"),
            P("dp"),
        ),
        out_specs=(
            P(("dp", "outer"), None, None),
            P(("dp", "outer"), None, None),
            P("dp"),
            P("dp"),
            P(None, "dp"),
            P("dp"),
            P("dp", None),
            P(),
            P("dp"),
            P("dp"),
            P("dp", None),
            P("dp"),
            P(None, "dp"),
            P("dp"),
        ),
        check_vma=False,
    )
```

profile of v0, /device:TPU:0, one launch (start us, length us, event | category | flops | bytes accessed | tf_op | source)
XLA Modules:
  0.0 606.7 jit_solution(15178385794157686121)
XLA Ops:
  17.9 79.6 %all-reduce.15 = (bf16[768]{0:T(1024)(128)(2,1)S(1)}, bf16[768]{0:T(1024)(128)(2,1)S(1)}, bf16[384]{0:T(512)(128)(2,1)S(1)}, bf16[768]{0:T(1024)(128)(2,1)S(1)},...) all-reduce(bf16[768]{0:T(1024)(128)(2,1)S(1)} %dynamic-update-slice, ...), channel_id=1, replica_groups=mesh['dp'=16,'outer'=2] {'dp'}, use_global_device_ids=true, to_apply=%add.1 | all-reduce | flops 7296 | bytes 29184
  99.2 37.8 %all_gather.57 = bf16[196,384]{0,1:T(8,128)(2,1)S(1)} all-gather(bf16[196,24]{0,1:T(8,128)(2,1)} %param.20), channel_id=1, replica_groups=mesh['dp'=16,'outer'=2] {'dp'}, dimensions={1}, use_global_device_ids=true | all-gather | bytes 159936 | tf_op jit(solution)/shard_map/all_gather | solution.py:72
  137.0 40.4 %all_gather.59 = bf16[384,196]{1,0:T(8,128)(2,1)S(1)} all-gather(bf16[24,196]{1,0:T(8,128)(2,1)} %param.22), channel_id=1, replica_groups=mesh['dp'=16,'outer'=2] {'dp'}, dimensions={0}, use_global_device_ids=true | all-gather | bytes 159936 | tf_op jit(solution)/shard_map/all_gather | solution.py:74
  183.1 9.7 %multiply_convert_fusion.1 = (bf16[12,768,384]{2,1,0:T(8,128)(2,1)S(1)}, f32[12,768,384]{2,1,0:T(8,128)}) fusion(f32[384]{0:T(512)S(1)} %convert_element_type.139, bf16[196,384]{0,1:T(8,128)(2,1)S(1)} %all_gather.57, bf16[12,196,768]{2,1,0:T(8,128)(2,1)S(1)} %copy-done, f32[768]{0:T(1024)S(1)} %convert_element_type.137, f32[768]{0:T(1024)S(1)} %convert_element_type.136, ...), kind=kOutput, calls=%fused_computation.21 | convolution fusion | flops 1433493504 | bytes 25023360 | tf_op jit(solution)/shard_map/isd,sk->idk/dot_general | solution.py:27
  192.9 3.4 fusion.66
  196.4 3.0 copy-done.4
  201.2 26.6 %multiply_convert_fusion = (bf16[12,196,3072]{2,1,0:T(8,128)(2,1)}, f32[12,196,3072]{2,1,0:T(8,128)}) fusion(f32[3072]{0:T(1024)S(1)} %convert_element_type.145, bf16[768,3072]{1,0:T(8,128)(2,1)} %all-gather.5.cloned.1.call-done, f32[12,196,768]{2,1,0:T(8,128)} %copy-done.4, f32[768]{0:T(1024)S(1)} %convert_element_type.143, ...), kind=kOutput, calls=%fused_computation.10 | convolution fusion | flops 11179413504 | bytes 55333248 | tf_op jit(solution)/shard_map/isd,dk->isk/dot_general | solution.py:39
  227.8 37.4 %convert_reduce_fusion = (f32[3072]{0:T(1024)}, bf16[12,196,3072]{2,1,0:T(8,128)(2,1)}) fusion(f32[12,196,3072]{2,1,0:T(8,128)} %get-tuple-element.95, f32[3072]{0:T(1024)S(1)} %convert_element_type.145, bf16[3072,768]{0,1:T(8,128)(2,1)} %all-gather.7.cloned.1.call-done, bf16[12,196,768]{2,1,0:T(8,128)(2,1)} %param.17, f32[12]{0:T(128)S(1)} %compare_convert_fusion), kind=kOutput, calls=%fused_computation.9 | convolution fusion | flops 11269727232 | bytes 51707952 | tf_op jit(solution)/shard_map/isd,kd->isk/dot_general | solution.py:115
  265.2 21.9 %bitcast_convert_fusion.1 = bf16[768,3072]{1,0:T(8,128)(2,1)} fusion(bf16[12,196,3072]{2,1,0:T(8,128)(2,1)} %get-tuple-element.102, f32[12,196,768]{2,1,0:T(8,128)} %copy-done.4, f32[768]{0:T(1024)S(1)} %convert_element_type.143, f32[768]{0:T(1024)S(1)} %convert_element_type.142, f32[12,196]{1,0:T(8,128)S(1)} %fusion.61, ...), kind=kOutput, calls=%fused_computation.32 | convolution fusion | flops 11109519360 | bytes 26419584 | tf_op jit(solution)/shard_map/isd,isk->dk/dot_general | solution.py:119
  287.2 20.2 %bitcast_convert_fusion = bf16[3072,768]{1,0:T(8,128)(2,1)} fusion(bf16[12,196,3072]{2,1,0:T(8,128)(2,1)} %get-tuple-element.94, bf16[12,196,768]{2,1,0:T(8,128)(2,1)} %param.17, f32[12]{0:T(128)S(1)} %compare_convert_fusion), kind=kOutput, calls=%fused_computation.31 | convolution fusion | flops 11105906688 | bytes 22782000 | tf_op jit(solution)/shard_map/isk,isd->kd/dot_general | solution.py:111
  310.2 19.6 %multiply_reduce_fusion = (f32[768]{0:T(1024)S(1)}, f32[12,196]{1,0:T(8,128)S(1)}, f32[768]{0:T(1024)S(1)}, f32[12,196,768]{2,1,0:T(8,128)S(1)}) fusion(f32[12,196,768]{2,1,0:T(8,128)} %copy-done.4, f32[12,196]{1,0:T(8,128)S(1)} %fusion.61, f32[12,196]{1,0:T(8,128)S(1)} %broadcast_multiply_fusion, f32[768]{0:T(1024)S(1)} %convert_element_type.142, ...), kind=kOutput, calls=%fused_computation.41 | convolution fusion | flops 11112574976 | bytes 33657408 | tf_op jit(solution)/shard_map/isk,dk->isd/dot_general | solution.py:123
  329.9 5.4 fusion.64
  338.3 3.6 convert_reduce_fusion.3
  341.9 4.6 copy.44
  346.6 16.8 %convert_reduce_fusion.1 = (f32[384]{0:T(512)}, bf16[12,768,384]{2,1,0:T(8,128)(2,1)S(1)}) fusion(f32[12,768,384]{2,1,0:T(8,128)} %get-tuple-element.91, f32[384]{0:T(512)S(1)} %copy-done.34, bf16[12,196,768]{2,1,0:T(8,128)(2,1)} %get-tuple-element.83, bf16[384,196]{1,0:T(8,128)(2,1)S(1)} %copy-done.13), kind=kOutput, calls=%fused_computation.20 | convolution fusion | flops 1468661376 | bytes 24999936 | tf_op jit(solution)/shard_map/isd,ks->idk/dot_general | solution.py:134
  370.8 3.8 fusion.62
  380.6 7.8 %fusion.26 = (f32[12,196]{1,0:T(8,128)S(1)}, f32[12,768,196]{1,2,0:T(8,128)S(1)}) fusion(bf16[12,196,768]{2,1,0:T(8,128)(2,1)} %param.15, f32[768]{0:T(1024)S(1)} %copy-done.23, f32[12,196]{1,0:T(8,128)S(1)} %copy-done.15, bf16[12,768,384]{2,1,0:T(8,128)(2,1)} %copy-done.8, bf16[196,384]{0,1:T(8,128)(2,1)S(1)} %copy-done.11), kind=kOutput, calls=%fused_computation.39 | convolution fusion | flops 1396295424 | bytes 18088320 | tf_op jit(solution)/shard_map/idk,sk->isd/dot_general | solution.py:142
  388.4 4.1 fusion.24
  392.6 18.9 %multiply_convert_fusion.2 = bf16[12,196,768]{2,1,0:T(8,128)(2,1)} fusion(f32[12,196,768]{2,1,0:T(8,128)} %copy-done.4, f32[768]{0:T(1024)S(1)} %copy-done.27, f32[12]{0:T(128)S(1)} %copy-done.30, bf16[12,196,3072]{2,1,0:T(8,128)(2,1)} %get-tuple-element.94, bf16[3072,768]{0,1:T(8,128)(2,1)} %all-gather.7.cloned.1.call-done), kind=kOutput, calls=%fused_computation.49 | convolution fusion | flops 11105353728 | bytes 30010416 | tf_op jit(solution)/shard_map/isk,kd->isd/dot_general | solution.py:86
  411.5 9.3 %fusion.27 = (f32[768]{0:T(1024)S(1)}, f32[12,196,768]{2,1,0:T(8,128)}) fusion(bf16[12,196,768]{2,1,0:T(8,128)(2,1)} %param.17, f32[12]{0:T(128)S(1)} %copy-done.30, f32[12,196]{1,0:T(8,128)S(1)} %negate_multiply_fusion, f32[12,196]{1,0:T(8,128)S(1)} %multiply_multiply_fusion.4, f32[12,196]{1,0:T(8,128)S(1)} %copy-done.15, ...), kind=kLoop, calls=%fused_computation.47 | loop fusion | flops 25287936 | bytes 28954608 | tf_op jit(solution)/shard_map/reduce_sum | solution.py:114
  420.7 3.6 reduce_sum.155
  424.4 38.0 %all-reduce.13 = (f32[768]{0:T(1024)S(1)}, f32[768]{0:T(1024)S(1)}, f32[384]{0:T(512)S(1)}, f32[196]{0:T(256)}, f32[768]{0:T(1024)S(1)}, /*index=5*/f32[768]{0:T(1024)S(1)}, f32[3072]{0:T(1024)S(1)}, f32[768]{0:T(1024)S(1)}) all-reduce(f32[768]{0:T(1024)S(1)} %get-tuple-element.58, ...), channel_id=1, replica_groups=mesh['dp'=16,'outer'=2] {'dp','outer'}, use_global_device_ids=true, to_apply=%region_9.0 | all-reduce | flops 7492 | bytes 59936 | tf_op jit(solution)/shard_map/psum | solution.py:182
  468.8 80.7 %all-reduce.18 = (bf16[98,384]{1,0:T(8,128)(2,1)S(1)}, bf16[384,98]{0,1:T(8,128)(2,1)S(1)}) all-reduce(f32[98,384]{1,0:T(8,128)S(1)} %dynamic-slice_convert_fusion.1, f32[384,98]{0,1:T(8,128)S(1)} %dynamic-slice_convert_fusion), channel_id=3, replica_groups=mesh['dp'=16,'outer'=2] {'dp'}, use_global_device_ids=true, to_apply=%region_13.0.clone | all-reduce | flops 75264 | bytes 451584
  558.0 36.7 %reduce-scatter.19.cloned.1.call-done = f32[48,1536]{1,0:T(8,128)} async-done(((f32[768,1536]{1,0:T(8,128)}), f32[48,1536]{1,0:T(8,128)}) %reduce-scatter.19.cloned.1.call-update) | async-done | bytes 294928
  (163 shorter events, 54.4 us)
Async XLA Ops:
  7.2 194.0 %all-gather.5.cloned.1.call-start = ((), (), s32[]{:S(2)}) async-start(), calls=%async_computation.4 | async-start | bytes 5013504 | tf_op jit(solution)/shard_map/all_gather | solution.py:79
  7.9 219.9 %all-gather.7.cloned.1.call-start = ((), (), s32[]{:S(2)}) async-start(), calls=%async_computation.5 | async-start | bytes 5013504 | tf_op jit(solution)/shard_map/all_gather | solution.py:81
  8.7 301.4 %reduce-scatter.13.cloned.1.call-start = ((), (), s32[]{:S(2)}) async-start(), calls=%async_computation.6 | async-start | bytes 7077888 | tf_op jit(solution)/shard_map/reduce_scatter | solution.py:155
  97.5 85.6 %copy-start = (bf16[12,196,768]{2,1,0:T(8,128)(2,1)S(1)}, bf16[12,196,768]{2,1,0:T(8,128)(2,1)}, u32[]{:S(2)}) copy-start(bf16[12,196,768]{2,1,0:T(8,128)(2,1)} %param.15) | copy-start | bytes 10838020
  97.5 95.3 %copy-start.22 = (f32[768]{0:T(1024)}, f32[768]{0:T(1024)S(1)}, u32[]{:S(2)}) copy-start(f32[768]{0:T(1024)S(1)} %convert_element_type.136) | copy-start | bytes 9220
  97.5 95.3 %copy-start.25 = (f32[768]{0:T(1024)}, f32[768]{0:T(1024)S(1)}, u32[]{:S(2)}) copy-start(f32[768]{0:T(1024)S(1)} %convert_element_type.137) | copy-start | bytes 9220
  97.5 95.3 %copy-start.33 = (f32[384]{0:T(512)}, f32[384]{0:T(512)S(1)}, u32[]{:S(2)}) copy-start(f32[384]{0:T(512)S(1)} %convert_element_type.139) | copy-start | bytes 4612
  137.0 55.9 %copy-start.10 = (bf16[196,384]{0,1:T(8,128)(2,1)}, bf16[196,384]{0,1:T(8,128)(2,1)S(1)}, u32[]{:S(2)}) copy-start(bf16[196,384]{0,1:T(8,128)(2,1)S(1)} %all_gather.57) | copy-start | bytes 451588
  177.4 157.9 %copy-start.29 = (f32[12]{0:T(128)}, f32[12]{0:T(128)S(1)}, u32[]{:S(2)}) copy-start(f32[12]{0:T(128)S(1)} %compare_convert_fusion) | copy-start | bytes 148
  287.2 54.7 %reduce-scatter.17.cloned.1.call-start = ((), (), s32[]{:S(2)}) async-start(), calls=%async_computation.8 | async-start | bytes 7077888 | tf_op jit(solution)/shard_map/reduce_scatter | solution.py:158
  287.2 20.3 %copy-start.35 = (u32[32]{0:T(128)S(1)}, u32[32]{0:T(128)}, u32[]{:S(2)}) copy-start(u32[32]{0:T(128)} %constant.104) | copy-start | bytes 388
  287.2 21.6 %copy-start.31 = (bf16[768]{0:T(1024)(128)(2,1)S(1)}, bf16[768]{0:T(1024)(128)(2,1)}, u32[]{:S(2)}) copy-start(bf16[768]{0:T(1024)(128)(2,1)} %get-tuple-element.77) | copy-start | bytes 4612
  307.5 247.3 %reduce-scatter.15.cloned.1.call-start = ((), (), s32[]{:S(2)}) async-start(), calls=%async_computation.7 | async-start | bytes 2506752 | tf_op jit(solution)/shard_map/reduce_scatter | solution.py:165
  310.1 19.7 %copy-start.21 = (f32[12,196]{1,0:T(8,128)S(1)}, f32[12,196]{1,0:T(8,128)}, u32[]{:S(2)}) copy-start(f32[12,196]{1,0:T(8,128)} %copy-done.20) | copy-start | bytes 28228
  310.1 284.5 %reduce-scatter.19.cloned.1.call-start = ((), (), s32[]{:S(2)}) async-start(), calls=%async_computation.9 | async-start | bytes 5013504
  346.5 20.5 %slice-start = ((s8[7077888]{0:T(1024)(128)(4,1)}), s8[2883584]{0:T(1024)(128)(4,1)S(1)}, s32[]{:S(2)}) async-start(s8[7077888]{0:T(1024)(128)(4,1)} %bitcast.101), calls=%async_computation.10 | async-start | bytes 5767168
  346.5 16.9 %copy-start.1 = (bf16[12,196,768]{2,1,0:T(8,128)(2,1)S(1)}, bf16[12,196,768]{2,1,0:T(8,128)(2,1)}, u32[]{:S(2)}) copy-start(bf16[12,196,768]{2,1,0:T(8,128)(2,1)} %param.15) | copy-start | bytes 10838020
  346.5 16.8 %copy-start.15 = (f32[12,196]{1,0:T(8,128)S(1)}, f32[12,196]{1,0:T(8,128)}, u32[]{:S(2)}) copy-start(f32[12,196]{1,0:T(8,128)} %copy-done.14) | copy-start | bytes 28228
  346.5 16.8 %copy-start.17 = (f32[12,196]{1,0:T(8,128)S(1)}, f32[12,196]{1,0:T(8,128)}, u32[]{:S(2)}) copy-start(f32[12,196]{1,0:T(8,128)} %copy-done.16) | copy-start | bytes 28228
  346.5 16.8 %copy-start.23 = (f32[768]{0:T(1024)S(1)}, f32[768]{0:T(1024)}, u32[]{:S(2)}) copy-start(f32[768]{0:T(1024)} %copy-done.22) | copy-start | bytes 9220
  346.6 20.4 %slice-start.1 = ((s8[7077888]{0:T(1024)(128)(4,1)}), s8[4194304]{0:T(1024)(128)(4,1)S(1)}, s32[]{:S(2)}) async-start(s8[7077888]{0:T(1024)(128)(4,1)} %bitcast.101), calls=%async_computation.11 | async-start | bytes 8388608
  375.2 91.3 %collective-permute-start.1 = (bf16[384,14]{0,1:T(8,128)(2,1)}, bf16[384,14]{0,1:T(8,128)(2,1)}, u32[]{:S(2)}, u32[]{:S(2)}) collective-permute-start(bf16[384,14]{0,1:T(8,128)(2,1)} %slice.1), channel_id=1, source_target_pairs={{0,1},{2,3},{4,5},{6,7},{8,9},{10,11},{12,13},{14,15},{16,17},{18,... | collective-permute-start | bytes 32264
  378.4 89.2 %collective-permute-start = (bf16[14,384]{1,0:T(8,128)(2,1)}, bf16[14,384]{1,0:T(8,128)(2,1)}, u32[]{:S(2)}, u32[]{:S(2)}) collective-permute-start(bf16[14,384]{1,0:T(8,128)(2,1)} %slice), channel_id=1, source_target_pairs={{0,1},{2,3},{4,5},{6,7},{8,9},{10,11},{12,13},{14,15},{16,17},{18,... | collective-permute-start | bytes 32264
  388.3 23.1 %copy-start.3 = (f32[12,768,196]{1,2,0:T(8,128)}, f32[12,768,196]{1,2,0:T(8,128)S(1)}, u32[]{:S(2)}) copy-start(f32[12,768,196]{1,2,0:T(8,128)S(1)} %get-tuple-element.98) | copy-start | bytes 21676036
  (22 other events, 152.5 us)
Sparse Core Ops, SparseCore 0:
  10.8 85.4 all-gather.4
  99.1 80.7 all-gather.6
  287.3 8.4 reduce-scatter.12
  307.6 8.4 reduce-scatter.16
  320.9 129.8 reduce-scatter.14
  456.6 138.0 reduce-scatter.18
where the time goes:
time: 617 us; the launch traced here: 607 us
  blocking collectives  288 us (47%)
  matrix products  188 us (30%)
  waiting for transfers between devices  38.2 us (6%)
  other arithmetic  35.1 us (6%)
  local copies, waits for them, and re-layouts  32.8 us (5%)
  between operations  19.4 us (3%)
    unnamed x3, blocking collectives  164 us
    all_gather x1, blocking collectives, on_device(): lax.all_gather(w_token_out, 'dp', axis=0, tiled=True)  40.4 us
    unnamed x9, waiting for transfers between devices  38.2 us
    psum x1, blocking collectives, on_device(): lax.psum((grad_gain_one, grad_shift_one, grad_tok_bin, grad_gain_two, gra...  38 us
    all_gather x1, blocking collectives, on_device(): lax.all_gather(w_token_in, 'dp', axis=1, tiled=True)  37.8 us
    dot_general x1, matrix products, on_device(): jnp.einsum('isd,kd->isk', d_chan_out, chan_wout, preferred_element_type=j...  37.4 us
    unnamed x103, local copies, waits for them, and re-layouts  27.3 us
    dot_general x1, matrix products, activations(): jnp.einsum('isd,dk->isk', chan_in, chan_win, preferred_element_type=jnp.f...  26.6 us
  transfers between devices with their start and end apart: 8, of which 1 were waited for; matrix products, arithmetic and copies ran while one was open for 31% of the time, Pallas kernels for 0%

commit v1 on v0

v1 whole, which is shorter than its diff:
```python
import functools

import jax
import jax.numpy as jnp
from jax import lax
from jax.experimental import pallas as pl
from jax.experimental.pallas import tpu as pltpu
from jax.sharding import PartitionSpec as P

EPS = 1e-06
F32 = jnp.float32
BF16 = jnp.bfloat16
NN = (((1,), (0,)), ((), ()))
NT = (((1,), (1,)), ((), ()))
TN = (((0,), (0,)), ((), ()))
ROOT = 0.7978845608028654
CUBE = 0.044715 * ROOT


def dot(left, right, dims):
    return lax.dot_general(left, right, dims, preferred_element_type=F32)


def gelu_both(value):
    square = value * value
    half = 0.5 + 0.5 * jnp.tanh(value * (ROOT + CUBE * square))
    slope = half + (half - half * half) * (value * (2 * ROOT + 6 * CUBE * square))
    return value * half, slope


def fold(values):
    return jnp.sum(values.reshape(values.shape[0] // 8, 8, values.shape[1]), axis=0)


def lane_mean(values):
    return jnp.mean(values, axis=-1, keepdims=True)


def standardize(values):
    centered = values - lane_mean(values)
    scale = lax.rsqrt(lane_mean(centered * centered) + EPS)
    return centered * scale, scale


def pad_rows(values, rows):
    extra = rows - values.shape[0]
    if extra == 0:
        return values
    return jnp.concatenate([values, jnp.zeros((extra, values.shape[1]), values.dtype)], axis=0)


class Sizes:
    def __init__(self, images, patches, channels, token_hidden, hidden, width, rows):
        self.images, self.patches, self.channels = images, patches, channels
        self.token_hidden, self.hidden, self.width = token_hidden, hidden, width
        self.padded = -(-patches // 8) * 8
        self.flat = images * self.padded
        self.blocks = hidden // width
        self.rows = rows
        self.chunks = self.flat // rows
        self.pairs = images // 2


def layer_kernel(
    sz,
    keep, patches, grad_out, weights,
    gain1, shift1, gain2, shift2, out_bias, tok_in_bias, tok_out_bias,
    tok_in_t, tok_in, tok_out_t, tok_out, chan_in_bias,
    mixed, grad_patches, kept_act, kept_slope, g_weights,
    g_gain1, g_shift1, g_gain2, g_shift2, g_out_bias, g_tok_in_bias, g_tok_out_bias,
    g_tok_in, g_tok_out, g_chan_in_bias,
    x_all, gout_all, chan_in, xhat2, scale2, masked, total_out, total_din,
    act_slot, slope_slot, act_s, dpre_s, w_slot, gw_slot, mixed_slot, gp_slot,
    load_sem, act_sem, w_sem, gw_sem, out_sem,
):
    pad, flat = sz.padded, sz.flat

    def load_copies(i):
        return (
            pltpu.make_async_copy(patches.at[i], x_all.at[i], load_sem.at[0, i]),
            pltpu.make_async_copy(grad_out.at[i], gout_all.at[i], load_sem.at[1, i]),
        )

    def weight_copies(j, slot):
        cols = pl.ds(pl.multiple_of(j * sz.width, sz.width), sz.width)
        return (
            pltpu.make_async_copy(weights.at[0, :, cols], w_slot.at[slot, 0], w_sem.at[slot, 0]),
            pltpu.make_async_copy(weights.at[1, :, cols], w_slot.at[slot, 1], w_sem.at[slot, 1]),
        )

    def grad_copies(j, slot):
        cols = pl.ds(pl.multiple_of(j * sz.width, sz.width), sz.width)
        return (
            pltpu.make_async_copy(gw_slot.at[slot, 0], g_weights.at[0, :, cols], gw_sem.at[slot, 0]),
            pltpu.make_async_copy(gw_slot.at[slot, 1], g_weights.at[1, :, cols], gw_sem.at[slot, 1]),
        )

    def keep_copies(pair, slot, k):
        i = pair * 2 + k
        return (
            pltpu.make_async_copy(act_slot.at[slot, k], kept_act.at[i], act_sem.at[slot, k, 0]),
            pltpu.make_async_copy(slope_slot.at[slot, k], kept_slope.at[i], act_sem.at[slot, k, 1]),
        )

    def back_copies(pair, slot, k):
        i = pair * 2 + k
        return (
            pltpu.make_async_copy(kept_act.at[i], act_slot.at[slot, k], act_sem.at[slot, k, 0]),
            pltpu.make_async_copy(kept_slope.at[i], slope_slot.at[slot, k], act_sem.at[slot, k, 1]),
        )

    def result_copies(pair, slot, k):
        i = pair * 2 + k
        return (
            pltpu.make_async_copy(mixed_slot.at[slot, k], mixed.at[i], out_sem.at[slot, k, 0]),
            pltpu.make_async_copy(gp_slot.at[slot, k], grad_patches.at[i], out_sem.at[slot, k, 1]),
        )

    def start(copies):
        for copy in copies:
            copy.start()

    def wait(copies):
        for copy in copies:
            copy.wait()

    def load_all(i, carry):
        start(load_copies(i))
        return carry

    lax.fori_loop(0, sz.images, load_all, 0)
    start(weight_copies(0, 0))
    for ref in (g_gain1, g_shift1, g_gain2, g_shift2, g_out_bias, g_tok_in_bias, g_tok_out_bias,
                g_tok_in, g_tok_out, g_chan_in_bias):
        ref[...] = jnp.zeros_like(ref)
    total_din[...] = jnp.zeros_like(total_din)

    def token_forward(pair, carry):
        slot = lax.rem(pair, 2)

        @pl.when(pair >= 2)
        def _():
            for k in range(2):
                wait(keep_copies(pair - 2, slot, k))

        residuals = []
        for k in range(2):
            i = pair * 2 + k
            wait(load_copies(i))
            x = pad_rows(x_all[i].astype(F32), pad)
            xhat, _ = standardize(x)
            token_in = (xhat * gain1[...] + shift1[...]).astype(BF16)
            pre = dot(tok_in_t[...], token_in, NN) + tok_in_bias[...]
            act, slope = gelu_both(pre)
            act = act.astype(BF16)
            act_slot[slot, k] = act
            slope_slot[slot, k] = slope.astype(BF16)
            residuals.append(x + dot(tok_out_t[...], act, NN) + tok_out_bias[...])
        both = pl.ds(pl.multiple_of(pair * 2 * pad, 16), 2 * pad)
        residual = jnp.concatenate(residuals, axis=0)
        hat, scale = standardize(residual)
        chan_in[both, :] = (hat * gain2[...] + shift2[...]).astype(BF16)
        xhat2[both, :] = hat.astype(BF16)
        scale2[both, :] = scale
        total_out[both, :] = residual + out_bias[...]
        cotangent = jnp.concatenate(
            [pad_rows(gout_all[pair * 2 + k].astype(F32), pad) * keep[pair * 2 + k] for k in range(2)], axis=0
        )
        masked[both, :] = cotangent.astype(BF16)
        g_out_bias[...] += fold(cotangent)
        for k in range(2):
            start(keep_copies(pair, slot, k))
        return carry

    lax.fori_loop(0, sz.pairs, token_forward, 0)
    for pair in range(max(0, sz.pairs - 2), sz.pairs):
        for k in range(2):
            wait(keep_copies(pair, pair % 2, k))

    def hidden_block(j, carry):
        slot = lax.rem(j, 2)
        wait(weight_copies(j, slot))

        @pl.when(j + 1 < sz.blocks)
        def _():
            start(weight_copies(j + 1, 1 - slot))

        def row_chunk(r, carry):
            rows = pl.ds(pl.multiple_of(r * sz.rows, 16), sz.rows)
            pre = dot(chan_in[rows, :], w_slot[slot, 0], NN) + chan_in_bias[j]
            d_act = dot(masked[rows, :], w_slot[slot, 1], NN)
            act, slope = gelu_both(pre)
            act = act.astype(BF16)
            d_pre = d_act * slope
            g_chan_in_bias[j] += fold(d_pre)
            d_pre = d_pre.astype(BF16)
            act_s[rows, :] = act
            dpre_s[rows, :] = d_pre
            total_out[rows, :] += dot(act, w_slot[slot, 1], NT)
            total_din[rows, :] += dot(d_pre, w_slot[slot, 0], NT)
            return carry

        lax.fori_loop(0, sz.chunks, row_chunk, 0)

        @pl.when(j >= 2)
        def _():
            wait(grad_copies(j - 2, slot))

        gw_slot[slot, 0] = dot(chan_in[...], dpre_s[...], TN)
        gw_slot[slot, 1] = dot(masked[...], act_s[...], TN)
        start(grad_copies(j, slot))
        return carry

    lax.fori_loop(0, sz.blocks, hidden_block, 0)
    for j in range(max(0, sz.blocks - 2), sz.blocks):
        wait(grad_copies(j, j % 2))
    for k in range(2):
        start(back_copies(0, 0, k))

    def token_backward(pair, carry):
        slot = lax.rem(pair, 2)

        @pl.when(pair + 1 < sz.pairs)
        def _():
            for k in range(2):
                start(back_copies(pair + 1, 1 - slot, k))

        @pl.when(pair >= 2)
        def _():
            for k in range(2):
                wait(result_copies(pair - 2, slot, k))

        both = pl.ds(pl.multiple_of(pair * 2 * pad, 16), 2 * pad)
        d_in = total_din[both, :]
        hat = xhat2[both, :].astype(F32)
        g_gain2[...] += fold(d_in * hat)
        g_shift2[...] += fold(d_in)
        e = d_in * gain2[...]
        d_residual = masked[both, :].astype(F32) + scale2[both, :] * (
            e - lane_mean(e) - hat * lane_mean(e * hat)
        )
        d_token_outs = d_residual.astype(BF16)
        rounded = d_token_outs.astype(F32)
        for k in range(2):
            i = pair * 2 + k
            part = slice(k * pad, (k + 1) * pad)
            wait(back_copies(pair, slot, k))
            d_token_out = rounded[part].astype(BF16)
            act = act_slot[slot, k]
            g_tok_out[...] += dot(act, d_token_out, NT)
            g_tok_out_bias[...] += jnp.sum(rounded[part], axis=-1, keepdims=True)
            d_pre = dot(tok_out[...], d_token_out, NN) * slope_slot[slot, k].astype(F32)
            g_tok_in_bias[...] += jnp.sum(d_pre, axis=-1, keepdims=True)
            d_pre = d_pre.astype(BF16)
            x = pad_rows(x_all[i].astype(F32), pad)
            hat1, scale1 = standardize(x)
            token_in = (hat1 * gain1[...] + shift1[...]).astype(BF16)
            g_tok_in[...] += dot(d_pre, token_in, NT)
            d_token_in = dot(tok_in[...], d_pre, NN)
            g_gain1[...] += fold(d_token_in * hat1)
            g_shift1[...] += fold(d_token_in)
            f = d_token_in * gain1[...]
            result = d_residual[part] + scale1 * (f - lane_mean(f) - hat1 * lane_mean(f * hat1))
            gp_slot[slot, k] = result[: sz.patches]
            layer = total_out[pl.ds(pl.multiple_of(i * pad, 8), pad), :] * keep[i]
            mixed_slot[slot, k] = layer[: sz.patches].astype(BF16)
            start(result_copies(pair, slot, k))
        return carry

    lax.fori_loop(0, sz.pairs, token_backward, 0)
    for pair in range(max(0, sz.pairs - 2), sz.pairs):
        for k in range(2):
            wait(result_copies(pair, pair % 2, k))


def run_layer(sz, keep, patches, grad_out, weights, small):
    shape = jax.ShapeDtypeStruct
    any_spec, vmem = pl.BlockSpec(memory_space=pl.ANY), pl.BlockSpec(memory_space=pltpu.VMEM)
    smem = pl.BlockSpec(memory_space=pltpu.SMEM)
    images, patch, pad, ch = sz.images, sz.patches, sz.padded, sz.channels
    row8 = shape((8, ch), F32)
    out_shape = (
        shape((images, patch, ch), BF16), shape((images, patch, ch), F32),
        shape((images, sz.token_hidden, ch), BF16), shape((images, sz.token_hidden, ch), BF16),
        shape((2, ch, sz.hidden), F32),
        row8, row8, row8, row8, row8,
        shape((sz.token_hidden, 1), F32), shape((pad, 1), F32),
        shape((sz.token_hidden, pad), F32), shape((sz.token_hidden, pad), F32),
        shape((sz.blocks, 8, sz.width), F32),
    )
    scratch = [
        pltpu.VMEM((images, patch, ch), BF16), pltpu.VMEM((images, patch, ch), BF16),
        pltpu.VMEM((sz.flat, ch), BF16), pltpu.VMEM((sz.flat, ch), BF16),
        pltpu.VMEM((sz.flat, 1), F32), pltpu.VMEM((sz.flat, ch), BF16),
        pltpu.VMEM((sz.flat, ch), F32), pltpu.VMEM((sz.flat, ch), F32),
        pltpu.VMEM((2, 2, sz.token_hidden, ch), BF16), pltpu.VMEM((2, 2, sz.token_hidden, ch), BF16),
        pltpu.VMEM((sz.flat, sz.width), BF16), pltpu.VMEM((sz.flat, sz.width), BF16),
        pltpu.VMEM((2, 2, ch, sz.width), BF16), pltpu.VMEM((2, 2, ch, sz.width), F32),
        pltpu.VMEM((2, 2, patch, ch), BF16), pltpu.VMEM((2, 2, patch, ch), F32),
        pltpu.SemaphoreType.DMA((2, images)), pltpu.SemaphoreType.DMA((2, 2, 2)),
        pltpu.SemaphoreType.DMA((2, 2)), pltpu.SemaphoreType.DMA((2, 2)),
        pltpu.SemaphoreType.DMA((2, 2, 2)),
    ]
    return pl.pallas_call(
        functools.partial(layer_kernel, sz),
        out_shape=out_shape,
        in_specs=[smem, any_spec, any_spec, any_spec] + [vmem] * 12,
        out_specs=[any_spec] * 5 + [vmem] * 10,
        scratch_shapes=scratch,
        compiler_params=pltpu.CompilerParams(vmem_limit_bytes=63 * 2**20),
    )(keep, patches, grad_out, weights, *small)


def on_device(
    patches, image_counts, grad_out,
    ln1_gain, ln1_bias, w_token_in, b_token_in, w_token_out, b_token_out,
    ln2_gain, ln2_bias, w_chan_in, b_chan_in, w_chan_out, b_chan_out,
):
    images, patch, ch = patches.shape
    token_part, hidden_part = b_token_in.shape[0], b_chan_in.shape[0]
    n_dp = lax.axis_size("dp")
    hidden = w_chan_in.shape[1]
    sz = Sizes(images, patch, ch, token_part * n_dp, hidden, 512, images * (-(-patch // 8) * 8) // 3)
    pad = sz.padded
    keep = (jnp.arange(images, dtype=jnp.int32) < image_counts[0]).astype(F32)

    weights = lax.all_gather(jnp.stack([w_chan_in, w_chan_out.T]), "dp", axis=1, tiled=True)
    tokens = lax.all_gather(jnp.stack([w_token_in.T, w_token_out]), "dp", axis=1, tiled=True)
    tokens = jnp.pad(tokens, ((0, 0), (0, 0), (0, pad - patch)))
    vectors = lax.all_gather(
        jnp.concatenate([ln1_gain, ln1_bias, ln2_gain, ln2_bias, b_chan_out, b_token_in, b_chan_in]), "dp", axis=0
    ).astype(F32)
    part = ch // n_dp
    whole = [vectors[:, k * part : (k + 1) * part].reshape(1, ch) for k in range(5)]
    tok_bias = vectors[:, 5 * part : 5 * part + token_part].reshape(-1, 1)
    chan_bias = vectors[:, 5 * part + token_part :].reshape(sz.blocks, 1, sz.width)
    out_bias = jnp.pad(b_token_out.astype(F32), (0, pad - patch))[:, None]
    small = (
        *whole, tok_bias, out_bias, tokens[0], tokens[0].T, tokens[1].T, tokens[1], chan_bias,
    )
    res = run_layer(sz, keep, patches, grad_out, weights, small)
    mixed, grad_patches, _, _, g_weights = res[:5]
    g_weights = lax.psum_scatter(g_weights.astype(BF16), ("dp",), scatter_dimension=1, tiled=True)
    g_weights = lax.psum(g_weights, "outer").astype(F32)
    g_tokens = jnp.stack([res[12], res[13]])
    g_tokens = lax.psum_scatter(g_tokens, ("dp",), scatter_dimension=1, tiled=True)
    g_tokens = lax.psum(g_tokens, "outer")[:, :, :patch]
    g_vec = lax.psum(
        tuple(jnp.sum(v, axis=0) for v in res[5:10])
        + (res[10][:, 0], res[11][:patch, 0], jnp.sum(res[14], axis=1).reshape(-1)),
        ("dp", "outer"),
    )

    def own(vector, length):
        return lax.dynamic_slice_in_dim(vector, lax.axis_index("dp") * length, length)

    return (
        mixed, grad_patches,
        own(g_vec[0], part), own(g_vec[1], part), g_tokens[0].T, own(g_vec[5], token_part), g_tokens[1], g_vec[6],
        own(g_vec[2], part), own(g_vec[3], part), g_weights[0], own(g_vec[7], hidden_part), g_weights[1].T,
        own(g_vec[4], part),
    )


def solution(mesh):
    slots = P(("dp", "outer"), None, None)
    return jax.shard_map(
        on_device,
        mesh=mesh,
        in_specs=(
            slots, P(("dp", "outer")), slots, P("dp"), P("dp"), P(None, "dp"), P("dp"), P("dp", None), P(),
            P("dp"), P("dp"), P("dp", None), P("dp"), P(None, "dp"), P("dp"),
        ),
        out_specs=(
            slots, slots, P("dp"), P("dp"), P(None, "dp"), P("dp"), P("dp", None), P(),
            P("dp"), P("dp"), P("dp", None), P("dp"), P(None, "dp"), P("dp"),
        ),
        check_vma=False,
    )
```

time: 617 us -> 607 us (0.984); the launches traced: 607 us -> 607 us
  waiting for transfers between devices: 38.2 us -> 264 us
  matrix products: 188 us -> 0 us
  Pallas kernels: 0 us -> 124 us
  blocking collectives: 288 us -> 166 us
  other arithmetic: 35.1 us -> 16.1 us
  local copies, waits for them, and re-layouts: 32.8 us -> 21.5 us
    reduce_scatter x3 -> x2, waiting for transfers between devices: 0.02 us -> 248 us  [the longest x1 166 us: on_device(): lax.psum_scatter(g_weights.astype(BF16), ('dp',), scatter_dimension=1, ti...]
    dot_general x12 -> x0, matrix products: 188 us -> none  [the longest x1 37.4 us: on_device(): jnp.einsum('isd,kd->isk', d_chan_out, chan_wout, preferred_element_type=j...]
    pallas_call x0 -> x1, Pallas kernels: none -> 124 us  [run_layer(): pl.pallas_call(functools.partial(layer_kernel, sz), out_shape=out_shape,...]
    unnamed x3 -> x1, blocking collectives: 164 us -> 80.3 us
    all_gather x6 -> x1, blocking collectives: 86.5 us -> 41.3 us  [on_device(): lax.all_gather(jnp.stack([w_token_in.T, w_token_out]), 'dp', axis=1, tile...]
    unnamed x9 -> x4, waiting for transfers between devices: 38.2 us -> 0.07 us
    reduce_sum x8 -> x6, other arithmetic: 32.7 us -> 0.1 us  [the longest x5 0.07 us: on_device(): jnp.sum(v, axis=0)]
    unnamed x103 -> x23, local copies, waits for them, and re-layouts: 27.3 us -> 2.49 us
  transfers between devices with their start and end apart: 8 -> 4, of which waited for: 1 -> 3; matrix products, arithmetic and copies ran while one was open for 31% -> 4% of each run, Pallas kernels for 0% -> 0%
where the time goes in v1:
time: 607 us
  waiting for transfers between devices  264 us (43%)
  blocking collectives  166 us (27%)
  Pallas kernels  124 us (20%)
  local copies, waits for them, and re-layouts  21.5 us (4%)
  other arithmetic  16.1 us (3%)
  between operations  15.3 us (3%)
    reduce_scatter x1, waiting for transfers between devices, on_device(): lax.psum_scatter(g_weights.astype(BF16), ('dp',), scatter_dimension=1, ti...  166 us
    pallas_call x1, Pallas kernels, run_layer(): pl.pallas_call(functools.partial(layer_kernel, sz), out_shape=out_shape,...  124 us
    reduce_scatter x1, waiting for transfers between devices, on_device(): lax.psum_scatter(g_tokens, ('dp',), scatter_dimension=1, tiled=True)  82.3 us
    unnamed x1, blocking collectives  80.3 us
    all_gather x1, blocking collectives, on_device(): lax.all_gather(jnp.stack([w_token_in.T, w_token_out]), 'dp', axis=1, tile...  41.3 us
    psum x1, blocking collectives, on_device(): lax.psum(tuple((jnp.sum(v, axis=0) for v in res[5:10])) + (res[10][:, 0],...  40.1 us
    psum x1, waiting for transfers between devices, on_device(): g_weights = lax.psum(g_weights, 'outer').astype(F32)  15.5 us
  transfers between devices with their start and end apart: 4, of which 3 were waited for; matrix products, arithmetic and copies ran while one was open for 4% of the time, Pallas kernels for 0%

profile of v1, /device:TPU:0, one launch (start us, length us, event | category | flops | bytes accessed | tf_op | source)
XLA Modules:
  0.0 606.5 jit_solution(5403525080464521994)
XLA Ops:
  7.2 1.9 pad_maximum_fusion.1
  9.2 1.2 dynamic-slice
  11.1 4.8 concatenate.3
  16.1 80.3 %all-reduce.2 = bf16[7296]{0:T(1024)(128)(2,1)S(1)} all-reduce(bf16[7296]{0:T(1024)(128)(2,1)S(1)} %dynamic-update-slice), channel_id=2, replica_groups=mesh['dp'=16,'outer'=2] {'dp'}, use_global_device_ids=true, to_apply=%add.2 | all-reduce | flops 7296 | bytes 29184
  96.8 0.7 reshape.52.gain1
  100.2 0.7 pad_maximum_fusion.2
  100.9 41.3 %all_gather.15 = bf16[2,384,196]{2,1,0:T(8,128)(2,1)S(1)} all-gather(bf16[2,24,196]{2,1,0:T(8,128)(2,1)S(1)} %pad_maximum_fusion.2), channel_id=1, replica_groups=mesh['dp'=16,'outer'=2] {'dp'}, dimensions={1}, use_global_device_ids=true | all-gather | bytes 319872 | tf_op jit(solution)/shard_map/all_gather | solution.py:328
  142.2 0.8 fusion.3
  143.0 0.8 copy.33.tok_in
  143.8 0.8 copy.34.tok_out_t
  144.6 0.8 reshape.68.tok_in_bias
  145.4 0.7 reshape.58.chan_in_bias
  146.7 0.8 copy.32.tok_out_bias
  148.7 123.7 %shard_map.254 = (bf16[12,196,768]{2,1,0:T(8,128)(2,1)}, f32[12,196,768]{2,1,0:T(8,128)}, bf16[12,384,768]{2,1,0:T(8,128)(2,1)}, bf16[12,384,768]{2,1,0:T(8,128)...) custom-call(f32[12]{0:T(128)} %compare_convert_fusion.keep, ...), custom_call_target="tpu_custom_call" | custom-call | tf_op jit(solution)/shard_map/pallas_call | solution.py:304
  272.4 9.9 %convert_element_type.19 = bf16[2,768,3072]{2,1,0:T(8,128)(2,1)} convert(f32[2,768,3072]{2,1,0:T(8,128)} %get-tuple-element.37) | non-fusion elementwise | flops 4718592 | bytes 28311552 | tf_op jit(solution)/shard_map/convert_element_type | solution.py:343
  282.5 0.8 copy-done
  283.4 0.9 pad_maximum_fusion
  284.4 166.0 %reduce-scatter.5.cloned.1.call-done = bf16[2,48,3072]{2,1,0:T(8,128)(2,1)} async-done(((bf16[2,768,3072]{2,1,0:T(8,128)(2,1)}), bf16[2,48,3072]{2,1,0:T(8,128)(2,1)}) %reduce-scatter.5.cloned.1.call-update) | async-done | bytes 589840 | tf_op jit(solution)/shard_map/reduce_scatter | solution.py:343
  450.9 40.1 %all-reduce.3 = (f32[768]{0:T(1024)S(1)}, f32[768]{0:T(1024)S(1)}, f32[384]{0:T(512)S(1)}, f32[196]{0:T(256)}, f32[768]{0:T(1024)S(1)}, /*index=5*/f32[768]{0:T(1024)S(1)}, f32[3072]{0:T(1024)S(1)}, f32[768]{0:T(1024)S(1)}) all-reduce(f32[768]{0:T(1024)S(1)} %reduce_sum.54, ...), channel_id=1, replica_groups=mesh['dp'=16,'outer'=2] {'dp','outer'}, use_global_device_ids=true, to_apply=%region_1.2 | all-reduce | flops 7492 | bytes 59936 | tf_op jit(solution)/shard_map/psum | solution.py:348
  495.2 82.3 %reduce-scatter.3.cloned.1.call-done = f32[2,24,200]{2,1,0:T(8,128)} async-done(((f32[2,384,200]{2,1,0:T(8,128)}), f32[2,24,200]{2,1,0:T(8,128)}) %reduce-scatter.3.cloned.1.call-update) | async-done | bytes 38416 | tf_op jit(solution)/shard_map/reduce_scatter | solution.py:346
  577.5 4.1 psum.72
  582.2 15.5 %all-reduce.6.cloned.1.call-done = bf16[2,48,3072]{2,1,0:T(8,128)(2,1)} async-done(((bf16[2,48,3072]{2,1,0:T(8,128)(2,1)}), bf16[2,48,3072]{2,1,0:T(8,128)(2,1)}) %all-reduce.6.cloned.1.call-update) | async-done | bytes 589840 | tf_op jit(solution)/shard_map/psum | solution.py:344
  597.7 1.2 convert_element_type.20
  598.9 1.1 slice_bitcast_fusion
  (57 shorter events, 9.9 us)
Async XLA Ops:
  7.2 141.5 %all-gather.3.cloned.1.call-start = ((), (), s32[]{:S(2)}) async-start(), calls=%async_computation.2 | async-start | bytes 10027008 | tf_op jit(solution)/shard_map/all_gather | solution.py:327
  9.2 441.3 %reduce-scatter.5.cloned.1.call-start = ((), (), s32[]{:S(2)}) async-start(), calls=%async_computation.4 | async-start | bytes 10027008 | tf_op jit(solution)/shard_map/reduce_scatter | solution.py:343
  282.3 1.0 copy-start
  282.3 1.1 copy-start.1
  282.3 168.1 %copy-start.4 = (f32[6,8,512]{2,1,0:T(8,128)S(1)}, f32[6,8,512]{2,1,0:T(8,128)}, u32[]{:S(2)}) copy-start(f32[6,8,512]{2,1,0:T(8,128)} %get-tuple-element.38) | copy-start | bytes 294916
  282.3 168.2 %copy-start.9 = (f32[8,768]{1,0:T(8,128)S(1)}, f32[8,768]{1,0:T(8,128)}, u32[]{:S(2)}) copy-start(f32[8,768]{1,0:T(8,128)} %get-tuple-element.29) | copy-start | bytes 73732
  282.3 168.2 %copy-start.8 = (f32[8,768]{1,0:T(8,128)S(1)}, f32[8,768]{1,0:T(8,128)}, u32[]{:S(2)}) copy-start(f32[8,768]{1,0:T(8,128)} %get-tuple-element.30) | copy-start | bytes 73732
  282.3 168.2 %copy-start.7 = (f32[8,768]{1,0:T(8,128)S(1)}, f32[8,768]{1,0:T(8,128)}, u32[]{:S(2)}) copy-start(f32[8,768]{1,0:T(8,128)} %get-tuple-element.35) | copy-start | bytes 73732
  282.3 168.3 %copy-start.6 = (f32[8,768]{1,0:T(8,128)S(1)}, f32[8,768]{1,0:T(8,128)}, u32[]{:S(2)}) copy-start(f32[8,768]{1,0:T(8,128)} %get-tuple-element.36) | copy-start | bytes 73732
  282.4 168.3 %copy-start.5 = (f32[8,768]{1,0:T(8,128)S(1)}, f32[8,768]{1,0:T(8,128)}, u32[]{:S(2)}) copy-start(f32[8,768]{1,0:T(8,128)} %get-tuple-element.39) | copy-start | bytes 73732
  282.4 168.3 %copy-start.2 = (f32[384,1]{1,0:T(8,128)S(1)}, f32[384,1]{1,0:T(8,128)}, u32[]{:S(2)}) copy-start(f32[384,1]{1,0:T(8,128)} %get-tuple-element.33) | copy-start | bytes 4612
  282.4 168.4 %copy-start.3 = (f32[200,1]{1,0:T(8,128)S(1)}, f32[200,1]{1,0:T(8,128)}, u32[]{:S(2)}) copy-start(f32[200,1]{1,0:T(8,128)} %get-tuple-element.34) | copy-start | bytes 2404
  282.4 295.1 %reduce-scatter.3.cloned.1.call-start = ((), (), s32[]{:S(2)}) async-start(), calls=%async_computation.3 | async-start | bytes 835584 | tf_op jit(solution)/shard_map/reduce_scatter | solution.py:346
  284.4 313.4 %all-reduce.6.cloned.1.call-start = ((), (), s32[]{:S(2)}) async-start(), calls=%async_computation.5 | async-start | bytes 1179648 | tf_op jit(solution)/shard_map/psum | solution.py:344
Sparse Core Ops, SparseCore 0:
  11.3 132.9 all-gather.2
  282.5 167.8 reduce-scatter.4
  455.8 121.5 reduce-scatter.2
  579.8 17.8 all-reduce.5

commit v2 on v1

v2 whole, which is shorter than its diff:
```python
import functools

import jax
import jax.numpy as jnp
from jax import lax
from jax.experimental import pallas as pl
from jax.experimental.pallas import tpu as pltpu
from jax.sharding import PartitionSpec as P

EPS = 1e-06
F32 = jnp.float32
BF16 = jnp.bfloat16
NN = (((1,), (0,)), ((), ()))
NT = (((1,), (1,)), ((), ()))
TN = (((0,), (0,)), ((), ()))
MESH = pl.DeviceIdType.MESH
ROOT = 0.7978845608028654
CUBE = 0.044715 * ROOT


def dot(left, right, dims):
    return lax.dot_general(left, right, dims, preferred_element_type=F32)


def gelu_both(value):
    square = value * value
    half = 0.5 + 0.5 * jnp.tanh(value * (ROOT + CUBE * square))
    slope = half + (half - half * half) * (value * (2 * ROOT + 6 * CUBE * square))
    return value * half, slope


def fold(values):
    return jnp.sum(values.reshape(values.shape[0] // 8, 8, values.shape[1]), axis=0)


def lane_mean(values):
    return jnp.mean(values, axis=-1, keepdims=True)


def standardize(values):
    centered = values - lane_mean(values)
    scale = lax.rsqrt(lane_mean(centered * centered) + EPS)
    return centered * scale, scale


def pad_rows(values, rows):
    extra = rows - values.shape[0]
    if extra == 0:
        return values
    return jnp.concatenate([values, jnp.zeros((extra, values.shape[1]), values.dtype)], axis=0)


class Sizes:
    def __init__(self, images, patches, channels, token_hidden, hidden, width, rows):
        self.images, self.patches, self.channels = images, patches, channels
        self.token_hidden, self.hidden, self.width = token_hidden, hidden, width
        self.padded = -(-patches // 8) * 8
        self.flat = images * self.padded
        self.blocks = hidden // width
        self.rows = rows
        self.chunks = self.flat // rows
        self.pairs = images // 2
        self.lanes = -(-self.padded // 128) * 128


def start(copies):
    for copy in copies:
        copy.start()


def wait(copies):
    for copy in copies:
        copy.wait()


class Place:
    def __init__(self):
        me, c = lax.axis_index("dp"), lax.axis_index("outer")
        z = me // 4
        yx = me - 4 * z
        y = yx // 2
        x = yx - 2 * y
        step_x, step_y = 1 - 2 * x, 2 * (1 - 2 * y)
        self.c, self.z, self.yx = c, z, yx
        self.yx_a = yx + (1 - c) * step_x + c * step_y
        self.yx_b = yx + c * step_x + (1 - c) * step_y
        self.yx_ab = yx + step_x + step_y
        self.sibling = (me, 1 - c)
        self.peer_a, self.peer_b = (4 * z + self.yx_a, c), (4 * z + self.yx_b, c)
        self.z_of = [lax.rem(z + k, 4) for k in range(4)]
        self.peer_z = [(4 * self.z_of[k] + yx, c) for k in range(4)]

    def greet(self):
        barrier = pltpu.get_barrier_semaphore()
        peers = [self.sibling, self.peer_a, self.peer_b] + self.peer_z[1:]
        for peer in peers:
            pl.semaphore_signal(barrier, inc=1, device_id=peer, device_id_type=MESH)
        pl.semaphore_wait(barrier, len(peers))


def remote(source, target, sems, index, peer):
    return pltpu.make_async_remote_copy(
        src_ref=source, dst_ref=target, send_sem=sems[0].at[index], recv_sem=sems[1].at[index],
        device_id=peer, device_id_type=MESH,
    )


class Gather:
    def __init__(self, place, own, view, sems, base):
        self.place, self.own, self.view, self.sems, self.base = place, own, view, sems, base

    def send(self, position, index, peer):
        ref = self.view(self.place.c, slice(None), position)
        return remote(ref, ref, self.sems, self.base + index, peer)

    @property
    def along_z(self):
        place = self.place
        target = self.view(place.c, place.z, place.yx)
        return [remote(self.own, target, self.sems, self.base + k - 1, place.peer_z[k]) for k in (1, 2, 3)]

    @property
    def along_a(self):
        return [self.send(self.place.yx, 3, self.place.peer_a)]

    @property
    def along_b(self):
        place = self.place
        return [self.send(place.yx, 4, place.peer_b), self.send(place.yx_a, 5, place.peer_b)]

    @property
    def swap(self):
        return [self.send(slice(None), 6, self.place.sibling)]

    def to_a(self):
        wait(self.along_z)
        start(self.along_a)

    def to_b(self):
        wait(self.along_a)
        start(self.along_b)

    def to_sibling(self):
        wait(self.along_b)
        start(self.swap)


class Reduce:
    def __init__(self, place, refs, own_out, sems, base, slot):
        (self.mine, csend, crecv, self.send1, self.keep1, recv1, self.send2, self.keep2, recv2,
         self.send3, self.keep3, recv3) = refs
        self.place, self.own_out, self.csend, self.sems, self.base = place, own_out, csend, sems, base
        self.crecv, self.recv1, self.recv2, self.recv3 = crecv.at[slot], recv1.at[slot], recv2.at[slot], recv3.at[slot]

    def send(self, source, target, index, peer):
        return remote(source, target, self.sems, self.base + index, peer)

    @property
    def swap(self):
        return [self.send(self.csend, self.crecv, 0, self.place.sibling)]

    @property
    def along_b(self):
        return [self.send(self.send1, self.recv1, 1, self.place.peer_b)]

    @property
    def along_a(self):
        return [self.send(self.send2, self.recv2, 2, self.place.peer_a)]

    @property
    def along_z(self):
        place = self.place
        return [
            self.send(self.send3.at[place.z_of[k]], self.recv3.at[k - 1], 2 + k, place.peer_z[k]) for k in (1, 2, 3)
        ]

    @property
    def finish(self):
        return [self.send(self.own_out, self.own_out, 6, self.place.sibling)]

    def to_b(self):
        wait(self.swap)
        place = self.place

        def step(z, carry):
            for q, (kept, sent) in enumerate(((place.yx, place.yx_b), (place.yx_a, place.yx_ab))):
                self.keep1[z, q] = self.mine[z, kept] + self.crecv[z, kept].astype(F32)
                self.send1[z, q] = (self.mine[z, sent] + self.crecv[z, sent].astype(F32)).astype(BF16)
            return carry

        lax.fori_loop(0, 4, step, 0)
        start(self.along_b)

    def to_a(self):
        wait(self.along_b)

        def step(z, carry):
            self.keep2[z] = self.keep1[z, 0] + self.recv1[z, 0].astype(F32)
            self.send2[z] = (self.keep1[z, 1] + self.recv1[z, 1].astype(F32)).astype(BF16)
            return carry

        lax.fori_loop(0, 4, step, 0)
        start(self.along_a)

    def to_z(self):
        wait(self.along_a)

        def step(z, carry):
            self.send3[z] = (self.keep2[z] + self.recv2[z].astype(F32)).astype(BF16)
            return carry

        lax.fori_loop(0, 4, step, 0)
        z = self.place.z
        self.keep3[...] = self.keep2[z] + self.recv2[z].astype(F32)
        start(self.along_z)

    def to_owner(self):
        wait(self.along_z)
        total = self.keep3[...]
        for k in range(3):
            total += self.recv3[k].astype(F32)
        self.own_out[...] = total
        start(self.finish)


def reduce_scratch(part, width, slots):
    return [
        pltpu.VMEM((4, 4, part, width), F32),
        pltpu.VMEM((4, 4, part, width), BF16), pltpu.VMEM((slots, 4, 4, part, width), BF16),
        pltpu.VMEM((4, 2, part, width), BF16), pltpu.VMEM((4, 2, part, width), F32),
        pltpu.VMEM((slots, 4, 2, part, width), BF16),
        pltpu.VMEM((4, part, width), BF16), pltpu.VMEM((4, part, width), F32),
        pltpu.VMEM((slots, 4, part, width), BF16),
        pltpu.VMEM((4, part, width), BF16), pltpu.VMEM((part, width), F32),
        pltpu.VMEM((slots, 3, part, width), BF16),
    ]


class Layer:
    def __init__(self, sz, **refs):
        self.sz = sz
        self.__dict__.update(refs)

    def load_copies(self, pair, k):
        i = pair * 2 + k
        return [pltpu.make_async_copy(self.patches.at[i], self.x_all.at[i], self.load_sem.at[i])]

    def cotangent_copies(self, pair, slot):
        return [
            pltpu.make_async_copy(self.grad_out.at[pair * 2 + k], self.mixed_slot.at[slot, k], self.out_sem.at[slot, k, 0])
            for k in range(2)
        ]

    def keep_copies(self, pair, slot, k):
        i = pair * 2 + k
        return [
            pltpu.make_async_copy(self.act_slot.at[slot, k], self.kept_act.at[i], self.act_sem.at[slot, k, 0]),
            pltpu.make_async_copy(self.slope_slot.at[slot, k], self.kept_slope.at[i], self.act_sem.at[slot, k, 1]),
        ]

    def back_copies(self, pair, slot):
        copies = []
        for k in range(2):
            i = pair * 2 + k
            copies += [
                pltpu.make_async_copy(self.kept_act.at[i], self.act_slot.at[slot, k], self.act_sem.at[slot, k, 0]),
                pltpu.make_async_copy(self.kept_slope.at[i], self.slope_slot.at[slot, k], self.act_sem.at[slot, k, 1]),
            ]
        return copies

    def result_copies(self, pair, slot, k):
        i = pair * 2 + k
        return [
            pltpu.make_async_copy(self.mixed_slot.at[slot, k], self.mixed.at[i], self.out_sem.at[slot, k, 0]),
            pltpu.make_async_copy(self.gp_slot.at[slot, k], self.grad_patches.at[i], self.out_sem.at[slot, k, 1]),
        ]

    def begin(self):
        def load_all(pair, carry):
            for k in range(2):
                start(self.load_copies(pair, k))
            return carry

        lax.fori_loop(0, self.sz.pairs, load_all, 0)
        start(self.cotangent_copies(0, 0))

    def clear(self):
        for ref in (self.g_gain1, self.g_shift1, self.g_gain2, self.g_shift2, self.g_out_bias, self.g_tok_out_bias,
                    self.g_tok, self.g_chan_in_bias):
            ref[...] = jnp.zeros_like(ref)

    def both(self, pair):
        return pl.ds(pl.multiple_of(pair * 2 * self.sz.padded, 16), 2 * self.sz.padded)

    def image(self, i):
        return pl.ds(pl.multiple_of(i * self.sz.padded, 8), self.sz.padded)

    def mask_pair(self, pair, carry):
        sz, slot = self.sz, lax.rem(pair, 2)

        @pl.when(pair + 1 < sz.pairs)
        def _():
            start(self.cotangent_copies(pair + 1, 1 - slot))

        wait(self.cotangent_copies(pair, slot))
        cotangent = jnp.concatenate(
            [pad_rows(self.mixed_slot[slot, k].astype(F32), sz.padded) * self.keep[pair * 2 + k] for k in range(2)],
            axis=0,
        )
        self.lhs[1, self.both(pair), :] = cotangent.astype(BF16)
        self.g_out_bias[...] += fold(cotangent)
        return carry

    def norm_pair(self, pair, carry):
        for k in range(2):
            wait(self.load_copies(pair, k))
            i = pair * 2 + k
            xhat, _ = standardize(pad_rows(self.x_all[i].astype(F32), self.sz.padded))
            self.total_din[self.image(i), :] = xhat
        return carry

    def token_input(self, xhat):
        sz = self.sz
        value = xhat * self.gain1[...] + self.shift1[...]
        row = lax.broadcasted_iota(jnp.int32, value.shape, 0)
        return jnp.where(row < sz.patches, value, jnp.where(row == sz.patches, 1.0, 0.0)).astype(BF16)

    def token_forward(self, pair):
        sz, slot = self.sz, lax.rem(pair, 2)

        @pl.when(pair >= 2)
        def _():
            for k in range(2):
                wait(self.keep_copies(pair - 2, slot, k))

        both = self.both(pair)
        residuals = []
        for k in range(2):
            i = pair * 2 + k
            token_in = self.token_input(self.total_din[self.image(i), :])
            act, slope = gelu_both(dot(self.tok_in_t[...], token_in, NN))
            act = act.astype(BF16)
            self.act_slot[slot, k] = act
            self.slope_slot[slot, k] = slope.astype(BF16)
            x = pad_rows(self.x_all[i].astype(F32), sz.padded)
            residuals.append(x + dot(self.tok_out_t[...], act, NN) + self.tok_out_bias[...])
        residual = jnp.concatenate(residuals, axis=0)
        hat, scale = standardize(residual)
        self.lhs[0, both, :] = (hat * self.gain2[...] + self.shift2[...]).astype(BF16)
        self.xhat2[both, :] = hat.astype(BF16)
        self.scale2[both, :] = scale
        self.total_out[both, :] = residual + self.out_bias[...]
        self.total_din[both, :] = jnp.zeros((2 * sz.padded, sz.channels), F32)
        for k in range(2):
            start(self.keep_copies(pair, slot, k))

    def token_forward_end(self):
        for pair in range(max(0, self.sz.pairs - 2), self.sz.pairs):
            for k in range(2):
                wait(self.keep_copies(pair, pair % 2, k))

    def row_chunk(self, j, slot, r):
        sz = self.sz
        rows = pl.ds(pl.multiple_of(r * sz.rows, 16), sz.rows)
        w_in = self.w_slot[slot, 0].reshape(sz.channels, sz.width)
        w_out = self.w_slot[slot, 1].reshape(sz.channels, sz.width)
        pre = dot(self.lhs[0, rows, :], w_in, NN) + self.chan_in_bias[j]
        d_act = dot(self.lhs[1, rows, :], w_out, NN)
        act, slope = gelu_both(pre)
        act = act.astype(BF16)
        d_pre = d_act * slope
        self.g_chan_in_bias[j] += fold(d_pre)
        d_pre = d_pre.astype(BF16)
        self.rhs[1, rows, :] = act
        self.rhs[0, rows, :] = d_pre
        self.total_out[rows, :] += dot(act, w_out, NT)
        self.total_din[rows, :] += dot(d_pre, w_in, NT)

    def weight_grad(self, matrix):
        return dot(self.lhs[matrix], self.rhs[matrix], TN)

    def token_backward(self, pair):
        sz, slot = self.sz, lax.rem(pair, 2)
        pad = sz.padded

        @pl.when(pair + 1 < sz.pairs)
        def _():
            start(self.back_copies(pair + 1, 1 - slot))

        @pl.when(pair >= 2)
        def _():
            for k in range(2):
                wait(self.result_copies(pair - 2, slot, k))

        both = self.both(pair)
        d_in = self.total_din[both, :]
        hat = self.xhat2[both, :].astype(F32)
        self.g_gain2[...] += fold(d_in * hat)
        self.g_shift2[...] += fold(d_in)
        e = d_in * self.gain2[...]
        d_residual = self.lhs[1, both, :].astype(F32) + self.scale2[both, :] * (
            e - lane_mean(e) - hat * lane_mean(e * hat)
        )
        rounded = d_residual.astype(BF16).astype(F32)
        wait(self.back_copies(pair, slot))
        for k in range(2):
            i = pair * 2 + k
            part = slice(k * pad, (k + 1) * pad)
            d_token_out = rounded[part].astype(BF16)
            self.g_tok[1] += dot(self.act_slot[slot, k], d_token_out, NT)
            self.g_tok_out_bias[...] += jnp.sum(rounded[part], axis=-1, keepdims=True)
            d_pre = dot(self.tok_out[...], d_token_out, NN) * self.slope_slot[slot, k].astype(F32)
            d_pre = d_pre.astype(BF16)
            hat1, scale1 = standardize(pad_rows(self.x_all[i].astype(F32), pad))
            self.g_tok[0] += dot(d_pre, self.token_input(hat1), NT)
            d_token_in = dot(self.tok_in[...], d_pre, NN)
            self.g_gain1[...] += fold(d_token_in * hat1)
            self.g_shift1[...] += fold(d_token_in)
            f = d_token_in * self.gain1[...]
            result = d_residual[part] + scale1 * (f - lane_mean(f) - hat1 * lane_mean(f * hat1))
            self.gp_slot[slot, k] = result[: sz.patches]
            layer = self.total_out[self.image(i), :] * self.keep[i]
            self.mixed_slot[slot, k] = layer[: sz.patches].astype(BF16)
            start(self.result_copies(pair, slot, k))

    def token_backward_end(self):
        for pair in range(max(0, self.sz.pairs - 2), self.sz.pairs):
            for k in range(2):
                wait(self.result_copies(pair, pair % 2, k))


def layer_scratch(sz, weight_shape):
    images, patch, ch = sz.images, sz.patches, sz.channels
    return dict(
        x_all=pltpu.VMEM((images, patch, ch), BF16),
        lhs=pltpu.VMEM((2, sz.flat, ch), BF16), xhat2=pltpu.VMEM((sz.flat, ch), BF16),
        scale2=pltpu.VMEM((sz.flat, 1), F32),
        total_out=pltpu.VMEM((sz.flat, ch), F32), total_din=pltpu.VMEM((sz.flat, ch), F32),
        act_slot=pltpu.VMEM((2, 2, sz.token_hidden, ch), BF16),
        slope_slot=pltpu.VMEM((2, 2, sz.token_hidden, ch), BF16),
        rhs=pltpu.VMEM((2, sz.flat, sz.width), BF16),
        w_slot=pltpu.VMEM((2, 2) + weight_shape + (sz.width,), BF16),
        mixed_slot=pltpu.VMEM((2, 2, patch, ch), BF16), gp_slot=pltpu.VMEM((2, 2, patch, ch), F32),
        load_sem=pltpu.SemaphoreType.DMA((images,)), act_sem=pltpu.SemaphoreType.DMA((2, 2, 2)),
        w_sem=pltpu.SemaphoreType.DMA((2, 2)), out_sem=pltpu.SemaphoreType.DMA((2, 2, 2)),
    )


def layer_sums(sz):
    ch = sz.channels
    return dict(
        g_gain1=((8, ch), F32), g_shift1=((8, ch), F32), g_gain2=((8, ch), F32), g_shift2=((8, ch), F32),
        g_out_bias=((8, ch), F32), g_tok_out_bias=((sz.padded, 1), F32),
        g_tok=((2, sz.token_hidden, sz.padded), F32), g_chan_in_bias=((sz.blocks, 8, sz.width), F32),
    )


def layer_params(sz):
    ch, pad, th = sz.channels, sz.padded, sz.token_hidden
    return dict(
        gain1=((1, ch), F32), shift1=((1, ch), F32), gain2=((1, ch), F32), shift2=((1, ch), F32),
        out_bias=((1, ch), F32), tok_in_t=((th, pad), BF16), tok_in=((pad, th), BF16),
        tok_out_t=((pad, th), BF16), tok_out=((th, pad), BF16), chan_in_bias=((sz.blocks, 1, sz.width), F32),
    )


def layer_results(sz):
    return dict(
        mixed=((sz.images, sz.patches, sz.channels), BF16),
        grad_patches=((sz.images, sz.patches, sz.channels), F32),
        kept_act=((sz.images, sz.token_hidden, sz.channels), BF16),
        kept_slope=((sz.images, sz.token_hidden, sz.channels), BF16),
    )


def call_kernel(kernel, inputs, outputs, scratch, **params):
    names = list(inputs) + list(outputs) + list(scratch)

    def body(*refs):
        kernel(dict(zip(names, refs)))

    results = pl.pallas_call(
        body,
        out_shape=[jax.ShapeDtypeStruct(*of) for of, _ in outputs.values()],
        in_specs=[spec for _, spec in inputs.values()],
        out_specs=[spec for _, spec in outputs.values()],
        scratch_shapes=list(scratch.values()),
        compiler_params=pltpu.CompilerParams(vmem_limit_bytes=63 * 2**20, **params),
    )(*[array for array, _ in inputs.values()])
    return dict(zip(outputs, results))


ANYWHERE = pl.BlockSpec(memory_space=pl.ANY)
VMEM = pl.BlockSpec(memory_space=pltpu.VMEM)
SMEM = pl.BlockSpec(memory_space=pltpu.SMEM)


def networked(sz, keep, patches, grad_out, own_weight, own_pack, tok_out_bias):
    part = sz.channels // 16
    tok_part = sz.token_hidden // 16
    pack_rows = own_pack.shape[0]
    blocks, width = sz.blocks, sz.width
    n_gather, n_reduce = blocks + 1, blocks + 1

    def kernel(refs):
        place = Place()
        layer = Layer(sz, **refs)
        gathered, pack_all = refs["gathered"], refs["pack_all"]
        gather_sems = (refs["gather_send"], refs["gather_recv"])
        reduce_sems = (refs["reduce_send"], refs["reduce_recv"])
        vector_sems = (refs["vector_send"], refs["vector_recv"])
        own_out, tok_fin = refs["own_out"], refs["tok_fin"]
        c = place.c
        chan_refs = [refs["chan_net_%d" % k] for k in range(12)]
        tok_refs = [refs["tok_net_%d" % k] for k in range(12)]

        def columns(j):
            return pl.ds(pl.multiple_of(j * width, width), width)

        def gather(j):
            cols = columns(j)

            def view(matrix, z, yx):
                return gathered.at[matrix, z, yx, :, cols]

            return Gather(place, refs["own_weight"].at[:, cols], view, gather_sems, j * 7)

        def pack_view(matrix, z, yx):
            return pack_all.at[matrix, z, yx]

        pack = Gather(place, refs["own_pack"], pack_view, gather_sems, blocks * 7)

        def reduce(j):
            return Reduce(place, chan_refs, own_out.at[c, :, columns(j)], reduce_sems, j * 7, lax.rem(j, 2))

        tok_reduce = Reduce(place, tok_refs, tok_fin.at[c], reduce_sems, blocks * 7, 0)
        own_copies = [
            pltpu.make_async_copy(refs["own_weight"], gathered.at[c, place.z, place.yx], refs["own_sem"].at[0]),
            pltpu.make_async_copy(refs["own_pack"], pack_all.at[c, place.z, place.yx], refs["own_sem"].at[1]),
        ]

        def weight_loads(j, slot):
            return [
                pltpu.make_async_copy(
                    gathered.at[m, :, :, :, columns(j)], layer.w_slot.at[slot, m], layer.w_sem.at[slot, m]
                )
                for m in range(2)
            ]

        start(own_copies)
        layer.begin()
        place.greet()
        start(pack.along_z)
        start(gather(0).along_z)
        layer.clear()
        lax.fori_loop(0, 2, layer.mask_pair, 0)
        wait(own_copies)
        pack.to_a()
        lax.fori_loop(2, sz.pairs, layer.mask_pair, 0)
        pack.to_b()
        gather(0).to_a()
        lax.fori_loop(0, sz.pairs // 2, layer.norm_pair, 0)
        pack.to_sibling()
        lax.fori_loop(sz.pairs // 2, sz.pairs, layer.norm_pair, 0)
        wait(pack.swap)
        start(gather(1).along_z)
        unpack(sz, layer, pack_all, tok_part)

        def forward_step(pair, carry):
            layer.token_forward(pair)

            @pl.when(pair == 0)
            def _():
                gather(0).to_b()
                gather(1).to_a()

            @pl.when(pair == 1)
            def _():
                start(gather(2).along_z)

            @pl.when(pair == 2)
            def _():
                gather(0).to_sibling()
                gather(1).to_b()

            @pl.when(pair == 3)
            def _():
                gather(2).to_a()
                start(gather(3).along_z)

            @pl.when(pair == 4)
            def _():
                wait(gather(0).swap)
                start(weight_loads(0, 0))
                gather(1).to_sibling()

            @pl.when(pair == 5)
            def _():
                gather(2).to_b()
                gather(3).to_a()
                start(gather(4).along_z)

            return carry

        lax.fori_loop(0, sz.pairs, forward_step, 0)
        layer.token_forward_end()

        def block_step(j, carry):
            slot = lax.rem(j, 2)
            wait(weight_loads(j, slot))

            def chunk(r, carry):
                layer.row_chunk(j, slot, r)

                @pl.when(r == 0)
                def _():
                    @pl.when(j >= 1)
                    def _():
                        reduce(j - 1).to_b()

                    @pl.when(j >= 2)
                    def _():
                        reduce(j - 2).to_z()

                @pl.when(r == 1)
                def _():
                    @pl.when(j + 1 < blocks)
                    def _():
                        wait(gather(j + 1).swap)
                        start(weight_loads(j + 1, 1 - slot))

                    @pl.when(j + 2 < blocks)
                    def _():
                        gather(j + 2).to_sibling()

                    @pl.when(j + 3 < blocks)
                    def _():
                        gather(j + 3).to_b()

                    @pl.when(j + 4 < blocks)
                    def _():
                        gather(j + 4).to_a()

                    @pl.when(j + 5 < blocks)
                    def _():
                        start(gather(j + 5).along_z)

                @pl.when(r == 2)
                def _():
                    @pl.when(j >= 1)
                    def _():
                        reduce(j - 1).to_a()

                    @pl.when(j >= 2)
                    def _():
                        reduce(j - 2).to_owner()

                return carry

            lax.fori_loop(0, sz.chunks, chunk, 0)
            mine, csend = chan_refs[0], chan_refs[1]
            csend[...] = layer.weight_grad(1 - c).astype(BF16).reshape(csend.shape)
            start(reduce(j).swap)
            mine[...] = layer.weight_grad(c).reshape(mine.shape)
            return carry

        lax.fori_loop(0, blocks, block_step, 0)
        start(layer.back_copies(0, 0))

        def backward_step(pair, carry):
            layer.token_backward(pair)

            @pl.when(pair == 0)
            def _():
                reduce(blocks - 1).to_b()
                reduce(blocks - 2).to_z()

            @pl.when(pair == 2)
            def _():
                reduce(blocks - 1).to_a()
                reduce(blocks - 2).to_owner()

            @pl.when(pair == 4)
            def _():
                reduce(blocks - 1).to_z()

            return carry

        lax.fori_loop(0, sz.pairs, backward_step, 0)

        mine, csend = tok_refs[0], tok_refs[1]

        def packed(matrix):
            value = layer.g_tok[matrix].reshape(16, tok_part, sz.padded)
            return value

        rows = pl.ds(0, tok_part)
        filler = jnp.zeros((16, pack_rows - tok_part, sz.padded), F32)
        for ref, matrix in ((csend, 1 - c), (mine, c)):
            value = jnp.concatenate([packed(matrix), filler], axis=1).astype(ref.dtype)
            ref[:, :, :, 0 : sz.padded] = value.reshape(4, 4, pack_rows, sz.padded)
            ref[:, :, :, sz.padded :] = jnp.zeros((4, 4, pack_rows, sz.lanes - sz.padded), ref.dtype)
            if ref is csend:
                start(tok_reduce.swap)
        vec, vec_in, vec_z = refs["vec"], refs["vec_in"], refs["vec_z"]
        vec[...] = jnp.zeros_like(vec)
        for k, ref in enumerate((layer.g_gain1, layer.g_shift1, layer.g_gain2, layer.g_shift2, layer.g_out_bias)):
            vec[k : k + 1, :] = jnp.sum(ref[...], axis=0, keepdims=True)
        for j in range(blocks):
            vec[5 + j : 6 + j, 0:width] = jnp.sum(layer.g_chan_in_bias[j], axis=0, keepdims=True)
        column = jnp.broadcast_to(layer.g_tok_out_bias[...], (sz.padded, 128))
        vec[5 + blocks : 6 + blocks, 0 : sz.padded] = jnp.transpose(column)[0:1]

        def vector_swap(k, peer):
            return [remote(vec, vec_in.at[k], vector_sems, k, peer)]

        swaps = [vector_swap(0, place.sibling), vector_swap(1, place.peer_a), vector_swap(2, place.peer_b)]
        vector_z = [remote(vec, vec_z.at[place.z], vector_sems, 2 + k, place.peer_z[k]) for k in (1, 2, 3)]

        def vector_add(k):
            wait(swaps[k])
            vec[...] += vec_in[k]

        start(swaps[0])
        reduce(blocks - 1).to_owner()
        vector_add(0)
        start(swaps[1])
        tok_reduce.to_b()
        vector_add(1)
        start(swaps[2])
        tok_reduce.to_a()
        vector_add(2)
        start(vector_z)
        vec_z[place.z] = vec[...]
        tok_reduce.to_z()
        layer.token_backward_end()
        wait(vector_z)
        refs["vec_out"][...] = (vec_z[0] + vec_z[1]) + (vec_z[2] + vec_z[3])
        tok_reduce.to_owner()

        def finish(j, carry):
            wait(reduce(j).finish)
            return carry

        lax.fori_loop(0, blocks, finish, 0)
        wait(tok_reduce.finish)

    inputs = dict(
        keep=(keep, SMEM), patches=(patches, ANYWHERE), grad_out=(grad_out, ANYWHERE),
        own_weight=(own_weight, ANYWHERE), own_pack=(own_pack, VMEM), tok_out_bias=(tok_out_bias, VMEM),
    )
    outputs = {name: (of, ANYWHERE) for name, of in layer_results(sz).items()}
    outputs["gathered"] = (((2, 4, 4, part, sz.hidden), BF16), ANYWHERE)
    outputs["own_out"] = (((2, part, sz.hidden), F32), VMEM)
    outputs["tok_fin"] = (((2, pack_rows, sz.lanes), F32), VMEM)
    outputs["vec_out"] = (((16, sz.channels), F32), VMEM)
    scratch = layer_scratch(sz, (4, 4, part))
    for group in (layer_sums(sz), layer_params(sz)):
        scratch.update({name: pltpu.VMEM(*of) for name, of in group.items()})
    scratch.update({"chan_net_%d" % k: of for k, of in enumerate(reduce_scratch(part, width, 2))})
    scratch.update({"tok_net_%d" % k: of for k, of in enumerate(reduce_scratch(pack_rows, sz.lanes, 1))})
    dma = pltpu.SemaphoreType.DMA
    scratch.update(
        pack_all=pltpu.VMEM((2, 4, 4, pack_rows, sz.lanes), BF16),
        vec=pltpu.VMEM((16, sz.channels), F32), vec_in=pltpu.VMEM((3, 16, sz.channels), F32),
        vec_z=pltpu.VMEM((4, 16, sz.channels), F32), own_sem=dma((2,)),
        gather_send=dma((n_gather * 7,)), gather_recv=dma((n_gather * 7,)),
        reduce_send=dma((n_reduce * 7,)), reduce_recv=dma((n_reduce * 7,)),
        vector_send=dma((6,)), vector_recv=dma((6,)),
    )
    return call_kernel(kernel, inputs, outputs, scratch, collective_id=0, has_side_effects=True)


def make_pack(sz, c, vectors, tok_in_part, tok_in_bias, tok_out_part, chan_bias):
    tok_part = tok_in_bias.shape[0]
    runs = sz.channels // 16 // tok_part
    cols = [vector.reshape(runs, tok_part).T for vector in vectors]
    first = jnp.concatenate(
        [tok_in_part.T, tok_in_bias[:, None], jnp.zeros((tok_part, sz.padded - sz.patches - 1), BF16)] + cols, axis=1
    )
    first = jnp.pad(first, ((0, 0), (0, sz.lanes - first.shape[1])))
    second = jnp.pad(tok_out_part, ((0, 0), (0, sz.lanes - sz.patches)))
    rows = -(-(tok_part + sz.hidden // sz.lanes // 2) // 16) * 16
    me = lax.broadcasted_iota(jnp.int32, (16, 1), 0) == lax.axis_index("dp")
    placed = jnp.where(me, chan_bias[None, :], jnp.zeros((), BF16)).reshape(-1, sz.lanes)
    half = placed.shape[0] // 2
    chosen = jnp.where(c == 0, first, second)
    bias = jnp.where(c == 0, placed[:half], placed[half:])
    return jnp.pad(jnp.concatenate([chosen, bias], axis=0), ((0, rows - tok_part - half), (0, 0)))


def unpack(sz, layer, pack_all, tok_part):
    pad, lanes, ch = sz.padded, sz.lanes, sz.channels
    rows = pack_all.shape[3]
    both = [pack_all[m].reshape(16, rows, lanes).astype(F32) for m in range(2)]
    first, second = (value[:, :tok_part].reshape(sz.token_hidden, lanes) for value in both)
    layer.tok_in_t[...] = first[:, :pad].astype(BF16)
    layer.tok_out[...] = second[:, :pad].astype(BF16)
    column = lax.broadcasted_iota(jnp.int32, first.shape, 1)
    layer.tok_in[...] = jnp.transpose(jnp.where(column < sz.patches, first, 0.0))[:pad].astype(BF16)
    layer.tok_out_t[...] = jnp.transpose(jnp.where(column < sz.patches, second, 0.0))[:pad].astype(BF16)
    runs = ch // 16 // tok_part
    shape = (16, tok_part, ch)
    device, row, lane = (lax.broadcasted_iota(jnp.int32, shape, k) for k in range(3))
    for v, ref in enumerate((layer.gain1, layer.shift1, layer.gain2, layer.shift2, layer.out_bias)):
        ref[...] = jnp.zeros_like(ref)
    for h in range(runs):
        place = lane == device * (runs * tok_part) + h * tok_part + row
        chosen = jnp.where(place, 1.0, 0.0).reshape(sz.token_hidden, ch).astype(BF16)
        spread = dot(first.astype(BF16), chosen, TN)
        for v, ref in enumerate((layer.gain1, layer.shift1, layer.gain2, layer.shift2, layer.out_bias)):
            index = pad + v * runs + h
            ref[...] += spread[index : index + 1]
    half = sz.hidden // lanes // 2
    bias = [jnp.sum(value[:, tok_part:], axis=0) for value in both]
    per_block = sz.width // lanes
    for j in range(sz.blocks):
        pieces = []
        for q in range(j * per_block, (j + 1) * per_block):
            pieces.append(bias[q // half][q % half : q % half + 1])
        layer.chan_in_bias[j] = jnp.concatenate(pieces, axis=1)


def local(sz, keep, patches, grad_out, weights, tok_out_bias, params):
    def kernel(refs):
        layer = Layer(sz, **refs)
        gw_slot, gw_sem = refs["gw_slot"], refs["gw_sem"]

        def columns(j):
            return pl.ds(pl.multiple_of(j * sz.width, sz.width), sz.width)

        def weight_loads(j, slot):
            return [
                pltpu.make_async_copy(refs["weights"].at[m, :, columns(j)], layer.w_slot.at[slot, m], layer.w_sem.at[slot, m])
                for m in range(2)
            ]

        def grad_stores(j, m):
            return [pltpu.make_async_copy(gw_slot.at[m], refs["g_weights"].at[m, :, columns(j)], gw_sem.at[m])]

        layer.begin()
        start(weight_loads(0, 0))
        layer.clear()
        lax.fori_loop(0, sz.pairs, layer.mask_pair, 0)
        lax.fori_loop(0, sz.pairs, layer.norm_pair, 0)

        def forward_step(pair, carry):
            layer.token_forward(pair)
            return carry

        lax.fori_loop(0, sz.pairs, forward_step, 0)
        layer.token_forward_end()

        def block_step(j, carry):
            slot = lax.rem(j, 2)
            wait(weight_loads(j, slot))

            @pl.when(j + 1 < sz.blocks)
            def _():
                start(weight_loads(j + 1, 1 - slot))

            def chunk(r, carry):
                layer.row_chunk(j, slot, r)
                return carry

            lax.fori_loop(0, sz.chunks, chunk, 0)
            for m in range(2):

                @pl.when(j >= 1)
                def _():
                    wait(grad_stores(j - 1, m))

                gw_slot[m] = layer.weight_grad(m)
                start(grad_stores(j, m))
            return carry

        lax.fori_loop(0, sz.blocks, block_step, 0)
        for m in range(2):
            wait(grad_stores(sz.blocks - 1, m))
        start(layer.back_copies(0, 0))

        def backward_step(pair, carry):
            layer.token_backward(pair)
            return carry

        lax.fori_loop(0, sz.pairs, backward_step, 0)
        layer.token_backward_end()

    inputs = dict(
        keep=(keep, SMEM), patches=(patches, ANYWHERE), grad_out=(grad_out, ANYWHERE), weights=(weights, ANYWHERE),
        tok_out_bias=(tok_out_bias, VMEM),
    )
    inputs.update({name: (params[name], VMEM) for name in layer_params(sz)})
    outputs = {name: (of, ANYWHERE) for name, of in layer_results(sz).items()}
    outputs["g_weights"] = (((2, sz.channels, sz.hidden), F32), ANYWHERE)
    outputs.update({name: (of, VMEM) for name, of in layer_sums(sz).items()})
    scratch = layer_scratch(sz, (sz.channels,))
    scratch.update(gw_slot=pltpu.VMEM((2, sz.channels, sz.width), F32), gw_sem=pltpu.SemaphoreType.DMA((2,)))
    return call_kernel(kernel, inputs, outputs, scratch)


def on_device(
    patches, image_counts, grad_out,
    ln1_gain, ln1_bias, w_token_in, b_token_in, w_token_out, b_token_out,
    ln2_gain, ln2_bias, w_chan_in, b_chan_in, w_chan_out, b_chan_out,
):
    images, patch, ch = patches.shape
    token_part, hidden_part, part = b_token_in.shape[0], b_chan_in.shape[0], ln1_gain.shape[0]
    n_dp = lax.axis_size("dp")
    hidden = w_chan_in.shape[1]
    sz = Sizes(images, patch, ch, token_part * n_dp, hidden, 512, images * (-(-patch // 8) * 8) // 3)
    pad = sz.padded
    keep = (jnp.arange(images, dtype=jnp.int32) < image_counts[0]).astype(F32)
    tok_out_bias = jnp.pad(b_token_out.astype(F32), (0, pad - patch))[:, None]
    vectors = (ln1_gain, ln1_bias, ln2_gain, ln2_bias, b_chan_out)

    def own(vector, length):
        return lax.dynamic_slice_in_dim(vector, lax.axis_index("dp") * length, length)

    if n_dp == 16 and sz.pairs == 6 and part % 16 == 0 and token_part % 8 == 0 and part % token_part == 0:
        c = lax.axis_index("outer")
        own_weight = jnp.where(c == 0, w_chan_in, w_chan_out.T)
        own_pack = make_pack(sz, c, vectors, w_token_in, b_token_in, w_token_out, b_chan_in)
        res = networked(sz, keep, patches, grad_out, own_weight, own_pack, tok_out_bias)
        g_weights, g_tokens, vec = res["own_out"], res["tok_fin"][:, :token_part], res["vec_out"]
        g_vec = [own(vec[k], part) for k in range(5)]
        g_chan_bias = own(vec[5 : 5 + sz.blocks, : sz.width].reshape(-1), hidden_part)
        g_tok_out_bias = vec[5 + sz.blocks, :patch]
    else:
        weights = lax.all_gather(jnp.stack([w_chan_in, w_chan_out.T]), "dp", axis=1, tiled=True)
        tokens = lax.all_gather(jnp.stack([w_token_in.T, w_token_out]), "dp", axis=1, tiled=True)
        tokens = jnp.pad(tokens, ((0, 0), (0, 0), (0, pad - patch)))
        every = lax.all_gather(jnp.concatenate(vectors + (b_token_in, b_chan_in)), "dp", axis=0)
        whole = [every[:, k * part : (k + 1) * part].reshape(1, ch).astype(F32) for k in range(5)]
        tok_bias = every[:, 5 * part : 5 * part + token_part].reshape(-1)
        params = dict(zip(("gain1", "shift1", "gain2", "shift2", "out_bias"), whole))
        params.update(
            tok_in_t=tokens[0].at[:, patch].set(tok_bias), tok_in=tokens[0].T,
            tok_out_t=tokens[1].T, tok_out=tokens[1],
            chan_in_bias=every[:, 5 * part + token_part :].reshape(sz.blocks, 1, sz.width).astype(F32),
        )
        res = local(sz, keep, patches, grad_out, weights, tok_out_bias, params)
        g_weights = lax.psum_scatter(res["g_weights"].astype(BF16), "dp", scatter_dimension=1, tiled=True)
        g_weights = lax.psum(g_weights, "outer").astype(F32)
        g_tokens = lax.psum(lax.psum_scatter(res["g_tok"], "dp", scatter_dimension=1, tiled=True), "outer")
        sums = [jnp.sum(res[name], axis=0) for name in ("g_gain1", "g_shift1", "g_gain2", "g_shift2", "g_out_bias")]
        sums += [jnp.sum(res["g_chan_in_bias"], axis=1).reshape(-1), res["g_tok_out_bias"][:patch, 0]]
        sums = lax.psum(tuple(sums), ("dp", "outer"))
        g_vec = [own(vector, part) for vector in sums[:5]]
        g_chan_bias, g_tok_out_bias = own(sums[5], hidden_part), sums[6]

    return (
        res["mixed"], res["grad_patches"],
        g_vec[0], g_vec[1], g_tokens[0, :, :patch].T, g_tokens[0, :, patch], g_tokens[1, :, :patch], g_tok_out_bias,
        g_vec[2], g_vec[3], g_weights[0], g_chan_bias, g_weights[1].T, g_vec[4],
    )


def solution(mesh):
    slots = P(("dp", "outer"), None, None)
    return jax.shard_map(
        on_device,
        mesh=mesh,
        in_specs=(
            slots, P(("dp", "outer")), slots, P("dp"), P("dp"), P(None, "dp"), P("dp"), P("dp", None), P(),
            P("dp"), P("dp"), P("dp", None), P("dp"), P(None, "dp"), P("dp"),
        ),
        out_specs=(
            slots, slots, P("dp"), P("dp"), P(None, "dp"), P("dp"), P("dp", None), P(),
            P("dp"), P("dp"), P("dp", None), P("dp"), P(None, "dp"), P("dp"),
        ),
        check_vma=False,
    )
```

time: 607 us -> 215 us (0.35)
  waiting for transfers between devices: 264 us -> 0 us
  blocking collectives: 166 us -> 0 us
  Pallas kernels: 124 us -> 183 us
  between operations: 15.3 us -> 1.35 us
  other arithmetic: 16.1 us -> 5.05 us
    reduce_scatter x2 -> x0, waiting for transfers between devices: 248 us -> none  [the longest x1 166 us: on_device(): lax.psum_scatter(g_weights.astype(BF16), ('dp',), scatter_dimension=1, ti...]
    unnamed x1 -> x0, blocking collectives: 80.3 us -> none
    pallas_call x1, Pallas kernels: 124 us -> 183 us  [call_kernel(): pl.pallas_call(body, out_shape=[jax.ShapeDtypeStruct(*of) for of, _ in ou...]
    psum x2 -> x0, blocking collectives: 44.3 us -> none  [the longest x1 40.1 us: on_device(): lax.psum(tuple((jnp.sum(v, axis=0) for v in res[5:10])) + (res[10][:, 0],...]
    all_gather x1 -> x0, blocking collectives: 41.3 us -> none  [on_device(): lax.all_gather(jnp.stack([w_token_in.T, w_token_out]), 'dp', axis=1, tile...]
    psum x1 -> x0, waiting for transfers between devices: 15.5 us -> none  [on_device(): g_weights = lax.psum(g_weights, 'outer').astype(F32)]
    convert_element_type x2 -> x0, other arithmetic: 11.1 us -> none  [the longest x1 9.92 us: on_device(): g_weights.astype(BF16)]
    unnamed x23 -> x4, local copies, waits for them, and re-layouts: 2.49 us -> 8.59 us
  transfers between devices with their start and end apart: 4 -> 0, of which waited for: 3 -> 0; matrix products, arithmetic and copies ran while one was open for 4% -> 0% of each run, Pallas kernels for 0% -> 0%
where the time goes in v2:
time: 215 us
  Pallas kernels  183 us (85%)
  local copies, waits for them, and re-layouts  25.7 us (12%)
  other arithmetic  5.05 us (2%)
    pallas_call x1, Pallas kernels, call_kernel(): pl.pallas_call(body, out_shape=[jax.ShapeDtypeStruct(*of) for of, _ in ou...  183 us
    unnamed x4, local copies, waits for them, and re-layouts  8.59 us

profile of v2, /device:TPU:0, one launch (start us, length us, event | category | flops | bytes accessed | tf_op | source)
XLA Modules:
  0.0 214.7 jit_solution(852096491924094333)
XLA Ops:
  0.7 0.7 broadcast_select_fusion
  1.5 0.7 reshape.62
  2.3 0.7 reshape.63
  3.2 0.7 reshape.64
  4.0 0.7 reshape.65
  4.9 0.7 reshape.66
  5.7 0.7 copy.40
  6.4 0.8 concatenate.6
  7.2 0.7 pad_select_fusion
  8.0 0.6 fusion.2.refs_4_
  8.6 1.8 bitcast_select_fusion.refs_3_
  10.4 0.7 pad_convert_fusion
  11.0 0.8 copy.41.refs_5_
  13.0 182.6 %shard_map.254 = (bf16[12,196,768]{2,1,0:T(8,128)(2,1)}, f32[12,196,768]{2,1,0:T(8,128)}, bf16[12,384,768]{2,1,0:T(8,128)(2,1)}, bf16[12,384,768]{2,1,0:T(8,128)...) custom-call(f32[12]{0:T(128)} %compare_convert_fusion.refs_0_, ...), custom_call_target="tpu_custom_call" | custom-call | tf_op jit(solution)/shard_map/pallas_call | solution.py:482
  195.6 0.9 fusion.8
  198.3 0.8 slice.59
  199.1 0.6 dynamic_slice.36
  199.7 1.4 slice_bitcast_fusion.2
  201.1 1.3 slice.55
  202.4 2.3 %slice_bitcast_fusion = (f32[3072,48]{0,1:T(8,128)}, f32[48,3072]{1,0:T(8,128)}) fusion(f32[2,48,3072]{2,1,0:T(8,128)} %get-tuple-element.23), kind=kLoop, calls=%fused_computation | loop fusion | bytes 2359296 | tf_op jit(solution)/shard_map/transpose | solution.py:955
  204.7 1.4 slice_reduce_fusion
  206.1 4.3 %copy.45 = bf16[12,196,768]{2,1,0:T(8,128)(2,1)} copy(bf16[12,196,768]{2,1,0:T(8,128)(2,1)} %get-tuple-element.51) | data formatting | bytes 7225344
  210.4 1.2 copy-done
  211.6 3.1 %copy.46 = f32[12,196,768]{2,1,0:T(8,128)} copy(f32[12,196,768]{2,1,0:T(8,128)S(1)} %copy-done) | data formatting | bytes 14450688
  (15 shorter events, 2.9 us)
Async XLA Ops:
  206.1 5.5 %copy-start = (f32[12,196,768]{2,1,0:T(8,128)S(1)}, f32[12,196,768]{2,1,0:T(8,128)}, u32[]{:S(2)}) copy-start(f32[12,196,768]{2,1,0:T(8,128)} %get-tuple-element.52) | copy-start | bytes 21676036

commit v3 on v2

v3 whole, which is shorter than its diff:
```python
import functools
import types

import jax
import jax.numpy as jnp
from jax import lax
from jax.experimental import pallas as pl
from jax.experimental.pallas import tpu as pltpu
from jax.sharding import PartitionSpec as P

EPS = 1e-06
F32 = jnp.float32
BF16 = jnp.bfloat16
NN = (((1,), (0,)), ((), ()))
NT = (((1,), (1,)), ((), ()))
TN = (((0,), (0,)), ((), ()))
MESH = pl.DeviceIdType.MESH
ROOT = 0.7978845608028654
CUBE = 0.044715 * ROOT


def dot(left, right, dims):
    return lax.dot_general(left, right, dims, preferred_element_type=F32)


def gelu_both(value):
    square = value * value
    half = 0.5 + 0.5 * jnp.tanh(value * (ROOT + CUBE * square))
    slope = half + (half - half * half) * (value * (2 * ROOT + 6 * CUBE * square))
    return value * half, slope


def fold(values):
    return jnp.sum(values.reshape(values.shape[0] // 8, 8, values.shape[1]), axis=0)


def lane_mean(values):
    return jnp.mean(values, axis=-1, keepdims=True)


def standardize(values):
    centered = values - lane_mean(values)
    scale = lax.rsqrt(lane_mean(centered * centered) + EPS)
    return centered * scale, scale


def pad_rows(values, rows):
    extra = rows - values.shape[0]
    if extra == 0:
        return values
    return jnp.concatenate([values, jnp.zeros((extra, values.shape[1]), values.dtype)], axis=0)


class Sizes:
    def __init__(self, images, patches, channels, token_hidden, hidden, width, rows):
        self.images, self.patches, self.channels = images, patches, channels
        self.token_hidden, self.hidden, self.width = token_hidden, hidden, width
        self.padded = -(-patches // 8) * 8
        self.flat = images * self.padded
        self.blocks = hidden // width
        self.rows = rows
        self.chunks = self.flat // rows
        self.pairs = images // 2
        self.lanes = -(-self.padded // 128) * 128


def start(copies):
    for copy in copies:
        copy.start()


def wait(copies):
    for copy in copies:
        copy.wait()


class Place:
    def __init__(self):
        me, c = lax.axis_index("dp"), lax.axis_index("outer")
        z = me // 4
        yx = me - 4 * z
        y = yx // 2
        x = yx - 2 * y
        step_x, step_y = 1 - 2 * x, 2 * (1 - 2 * y)
        self.c, self.z, self.yx = c, z, yx
        self.yx_a = yx + (1 - c) * step_x + c * step_y
        self.yx_b = yx + c * step_x + (1 - c) * step_y
        self.yx_ab = yx + step_x + step_y
        self.sibling = (me, 1 - c)
        self.peer_a, self.peer_b = (4 * z + self.yx_a, c), (4 * z + self.yx_b, c)
        self.z_of = [lax.rem(z + k, 4) for k in range(4)]
        self.peer_z = [(4 * self.z_of[k] + yx, c) for k in range(4)]
        self.peers_xy = [self.peer_a, self.peer_b, (4 * z + self.yx_ab, c)]
        self.yx_xy = [self.yx_a, self.yx_b, self.yx_ab]

    def greet(self):
        barrier = pltpu.get_barrier_semaphore()
        peers = [self.sibling] + self.peers_xy + self.peer_z[1:]
        for peer in peers:
            pl.semaphore_signal(barrier, inc=1, device_id=peer, device_id_type=MESH)
        pl.semaphore_wait(barrier, len(peers))


def remote(source, target, sems, index, peer):
    return pltpu.make_async_remote_copy(
        src_ref=source, dst_ref=target, send_sem=sems[0].at[index], recv_sem=sems[1].at[index],
        device_id=peer, device_id_type=MESH,
    )


class Gather:
    def __init__(self, place, own, view, sems, base):
        self.place, self.own, self.view, self.sems, self.base = place, own, view, sems, base

    def send(self, position, index, peer):
        ref = self.view(self.place.c, slice(None), position)
        return remote(ref, ref, self.sems, self.base + index, peer)

    @property
    def along_z(self):
        place = self.place
        target = self.view(place.c, place.z, place.yx)
        return [remote(self.own, target, self.sems, self.base + k - 1, place.peer_z[k]) for k in (1, 2, 3)]

    @property
    def along_a(self):
        return [self.send(self.place.yx, 3, self.place.peer_a)]

    @property
    def along_b(self):
        place = self.place
        return [self.send(place.yx, 4, place.peer_b), self.send(place.yx_a, 5, place.peer_b)]

    @property
    def along_xy(self):
        place = self.place
        return [self.send(place.yx, 3 + k, place.peers_xy[k]) for k in range(3)]

    @property
    def swap(self):
        return [self.send(slice(None), 6, self.place.sibling)]

    def to_xy(self):
        wait(self.along_z)
        start(self.along_xy)

    def xy_to_sibling(self):
        wait(self.along_xy)
        start(self.swap)

    def to_a(self):
        wait(self.along_z)
        start(self.along_a)

    def to_b(self):
        wait(self.along_a)
        start(self.along_b)

    def to_sibling(self):
        wait(self.along_b)
        start(self.swap)


class Reduce:
    def __init__(self, place, refs, own_out, sems, base, slot):
        (self.mine, csend, crecv, self.send1, self.keep1, recv1, self.send2, self.keep2, recv2,
         self.send3, self.keep3, recv3) = refs
        self.place, self.own_out, self.csend, self.sems, self.base = place, own_out, csend, sems, base
        self.crecv, self.recv1, self.recv2, self.recv3 = crecv.at[slot], recv1.at[slot], recv2.at[slot], recv3.at[slot]

    def send(self, source, target, index, peer):
        return remote(source, target, self.sems, self.base + index, peer)

    @property
    def swap(self):
        return [self.send(self.csend, self.crecv, 0, self.place.sibling)]

    @property
    def along_b(self):
        return [self.send(self.send1, self.recv1, 1, self.place.peer_b)]

    @property
    def along_a(self):
        return [self.send(self.send2, self.recv2, 2, self.place.peer_a)]

    @property
    def along_z(self):
        place = self.place
        return [
            self.send(self.send3.at[place.z_of[k]], self.recv3.at[k - 1], 2 + k, place.peer_z[k]) for k in (1, 2, 3)
        ]

    @property
    def finish(self):
        return [self.send(self.own_out, self.own_out, 6, self.place.sibling)]

    def to_b(self):
        wait(self.swap)
        place = self.place

        def step(z, carry):
            for q, (kept, sent) in enumerate(((place.yx, place.yx_b), (place.yx_a, place.yx_ab))):
                self.keep1[z, q] = (self.mine[z, kept].astype(F32) + self.crecv[z, kept].astype(F32)).astype(BF16)
                self.send1[z, q] = (self.mine[z, sent].astype(F32) + self.crecv[z, sent].astype(F32)).astype(BF16)
            return carry

        lax.fori_loop(0, 4, step, 0)
        start(self.along_b)

    def to_a(self):
        wait(self.along_b)

        def step(z, carry):
            self.keep2[z] = self.keep1[z, 0].astype(F32) + self.recv1[z, 0].astype(F32)
            self.send2[z] = (self.keep1[z, 1].astype(F32) + self.recv1[z, 1].astype(F32)).astype(BF16)
            return carry

        lax.fori_loop(0, 4, step, 0)
        start(self.along_a)

    def to_z(self):
        wait(self.along_a)

        def step(z, carry):
            self.send3[z] = (self.keep2[z] + self.recv2[z].astype(F32)).astype(BF16)
            return carry

        lax.fori_loop(0, 4, step, 0)
        z = self.place.z
        self.keep3[...] = self.keep2[z] + self.recv2[z].astype(F32)
        start(self.along_z)

    def to_owner(self):
        wait(self.along_z)
        total = self.keep3[...]
        for k in range(3):
            total += self.recv3[k].astype(F32)
        self.own_out[...] = total
        start(self.finish)


class SmallReduce:
    def __init__(self, place, refs, own_out, sems):
        self.mine, self.csend, self.crecv, self.send1, self.keep1, self.recv1, self.send3, self.keep3, self.recv3 = refs
        self.place, self.own_out, self.sems = place, own_out, sems

    def send(self, source, target, index, peer):
        return remote(source, target, self.sems, index, peer)

    @property
    def swap(self):
        return [self.send(self.csend, self.crecv, 0, self.place.sibling)]

    @property
    def along_xy(self):
        place = self.place
        return [self.send(self.send1.at[k], self.recv1.at[k], 1 + k, place.peers_xy[k]) for k in range(3)]

    @property
    def along_z(self):
        place = self.place
        return [
            self.send(self.send3.at[place.z_of[k]], self.recv3.at[k - 1], 3 + k, place.peer_z[k]) for k in (1, 2, 3)
        ]

    @property
    def finish(self):
        return [self.send(self.own_out, self.own_out, 7, self.place.sibling)]

    def to_xy(self):
        wait(self.swap)
        place = self.place
        for k in range(3):
            at = place.yx_xy[k]
            self.send1[k] = (self.mine[:, at] + self.crecv[:, at].astype(F32)).astype(BF16)
        start(self.along_xy)
        self.keep1[...] = self.mine[:, place.yx] + self.crecv[:, place.yx].astype(F32)

    def to_z(self):
        wait(self.along_xy)
        total = self.keep1[...]
        for k in range(3):
            total += self.recv1[k].astype(F32)
        self.send3[...] = total.astype(BF16)
        start(self.along_z)
        self.keep1[...] = total
        self.keep3[...] = self.keep1[self.place.z]

    def to_owner(self):
        wait(self.along_z)
        total = self.keep3[...]
        for k in range(3):
            total += self.recv3[k].astype(F32)
        self.own_out[...] = total
        start(self.finish)


def small_reduce_scratch(part, width):
    return [
        pltpu.VMEM((4, 4, part, width), F32),
        pltpu.VMEM((4, 4, part, width), BF16), pltpu.VMEM((4, 4, part, width), BF16),
        pltpu.VMEM((3, 4, part, width), BF16), pltpu.VMEM((4, part, width), F32),
        pltpu.VMEM((3, 4, part, width), BF16),
        pltpu.VMEM((4, part, width), BF16), pltpu.VMEM((part, width), F32),
        pltpu.VMEM((3, part, width), BF16),
    ]


def reduce_scratch(part, width, slots):
    return [
        pltpu.VMEM((4, 4, part, width), BF16),
        pltpu.VMEM((4, 4, part, width), BF16), pltpu.VMEM((slots, 4, 4, part, width), BF16),
        pltpu.VMEM((4, 2, part, width), BF16), pltpu.VMEM((4, 2, part, width), BF16),
        pltpu.VMEM((slots, 4, 2, part, width), BF16),
        pltpu.VMEM((4, part, width), BF16), pltpu.VMEM((4, part, width), F32),
        pltpu.VMEM((slots, 4, part, width), BF16),
        pltpu.VMEM((4, part, width), BF16), pltpu.VMEM((part, width), F32),
        pltpu.VMEM((slots, 3, part, width), BF16),
    ]


class Layer:
    def __init__(self, sz, refs):
        self.sz = sz
        self.__dict__.update(vars(refs))

    def load_copies(self, pair, slot):
        return [
            pltpu.make_async_copy(self.patches.at[pair * 2 + k], self.x_slot.at[slot, k], self.load_sem.at[slot, k])
            for k in range(2)
        ]

    def next_images(self, pair):
        slot = lax.rem(pair, 2)
        following = jnp.where(pair + 1 < self.sz.pairs, pair + 1, 0)
        start(self.load_copies(following, 1 - slot))
        wait(self.load_copies(pair, slot))

    def image_of(self, pair, k):
        return pad_rows(self.x_slot[lax.rem(pair, 2), k].astype(F32), self.sz.padded)

    def cotangent_copies(self, pair, slot):
        return [
            pltpu.make_async_copy(self.grad_out.at[pair * 2 + k], self.mixed_slot.at[slot, k], self.out_sem.at[slot, k, 0])
            for k in range(2)
        ]

    def keep_copies(self, pair, slot, k):
        i = pair * 2 + k
        return [
            pltpu.make_async_copy(self.act_slot.at[slot, k], self.kept_act.at[i], self.act_sem.at[slot, k, 0]),
            pltpu.make_async_copy(self.slope_slot.at[slot, k], self.kept_slope.at[i], self.act_sem.at[slot, k, 1]),
        ]

    def back_copies(self, pair, slot):
        copies = []
        for k in range(2):
            i = pair * 2 + k
            copies += [
                pltpu.make_async_copy(self.kept_act.at[i], self.act_slot.at[slot, k], self.act_sem.at[slot, k, 0]),
                pltpu.make_async_copy(self.kept_slope.at[i], self.slope_slot.at[slot, k], self.act_sem.at[slot, k, 1]),
            ]
        return copies

    def result_copies(self, pair, slot, k):
        i = pair * 2 + k
        return [
            pltpu.make_async_copy(self.gp_slot.at[slot, k], self.grad_patches.at[i], self.out_sem.at[slot, k, 1]),
        ]

    def begin(self):
        start(self.load_copies(0, 0))
        start(self.cotangent_copies(0, 0))

    def clear(self):
        for ref in (self.g_gain1, self.g_shift1, self.g_gain2, self.g_shift2, self.g_out_bias, self.g_tok_out_bias,
                    self.g_tok, self.g_chan_in_bias):
            ref[...] = jnp.zeros_like(ref)

    def kept(self, i):
        return jnp.where(i < self.counts[0], 1.0, 0.0)

    def both(self, pair):
        return pl.ds(pl.multiple_of(pair * 2 * self.sz.padded, 16), 2 * self.sz.padded)

    def image(self, i):
        return pl.ds(pl.multiple_of(i * self.sz.padded, 8), self.sz.padded)

    def mask_pair(self, pair, carry):
        sz, slot = self.sz, lax.rem(pair, 2)

        @pl.when(pair + 1 < sz.pairs)
        def _():
            start(self.cotangent_copies(pair + 1, 1 - slot))

        wait(self.cotangent_copies(pair, slot))
        cotangent = jnp.concatenate(
            [pad_rows(self.mixed_slot[slot, k].astype(F32), sz.padded) * self.kept(pair * 2 + k) for k in range(2)],
            axis=0,
        )
        self.lhs[1, self.both(pair), :] = cotangent.astype(BF16)
        self.g_out_bias[...] += fold(cotangent)
        return carry

    def norm_pair(self, pair, carry):
        self.next_images(pair)
        for k in range(2):
            xhat, _ = standardize(self.image_of(pair, k))
            self.total_din[self.image(pair * 2 + k), :] = xhat
        return carry

    def token_input(self, xhat):
        patch = self.sz.patches
        value = xhat * self.gain1[...] + self.shift1[...]
        whole = patch // 8 * 8
        rest = value[whole:]
        row = lax.broadcasted_iota(jnp.int32, rest.shape, 0) + whole
        rest = jnp.where(row < patch, rest, jnp.where(row == patch, 1.0, 0.0))
        return jnp.concatenate([value[:whole], rest], axis=0).astype(BF16)

    def token_forward(self, pair):
        sz, slot = self.sz, lax.rem(pair, 2)

        @pl.when(pair >= 2)
        def _():
            for k in range(2):
                wait(self.keep_copies(pair - 2, slot, k))

        self.next_images(pair)
        both = self.both(pair)
        residuals = []
        for k in range(2):
            i = pair * 2 + k
            token_in = self.token_input(self.total_din[self.image(i), :])
            act, slope = gelu_both(dot(self.tok_in_t[...], token_in, NN))
            act = act.astype(BF16)
            self.act_slot[slot, k] = act
            self.slope_slot[slot, k] = slope.astype(BF16)
            residuals.append(self.image_of(pair, k) + dot(self.tok_out_t[...], act, NN) + self.tok_out_bias[...])
        residual = jnp.concatenate(residuals, axis=0)
        hat, scale = standardize(residual)
        self.lhs[0, both, :] = (hat * self.gain2[...] + self.shift2[...]).astype(BF16)
        self.xhat2[both, :] = hat.astype(BF16)
        lane = lax.broadcasted_iota(jnp.int32, self.scale2.shape, 1)
        self.scale2[...] = jnp.where(lane == pair, scale, self.scale2[...])
        self.total_out[both, :] = residual + self.out_bias[...]
        self.total_din[both, :] = jnp.zeros((2 * sz.padded, sz.channels), F32)
        for k in range(2):
            start(self.keep_copies(pair, slot, k))

    def token_forward_end(self):
        for pair in range(max(0, self.sz.pairs - 2), self.sz.pairs):
            for k in range(2):
                wait(self.keep_copies(pair, pair % 2, k))

    def weights_of(self, slot, matrix):
        return self.w_slot[slot, matrix].reshape(self.sz.channels, self.sz.width)

    def row_chunk(self, j, slot, r, late):
        sz = self.sz
        rows = pl.ds(pl.multiple_of(r * sz.rows, 16), sz.rows)
        w_in, w_out = self.weights_of(slot, 0), self.weights_of(slot, 1)
        pre = dot(self.lhs[0, rows, :], w_in, NN) + self.chan_in_bias[j]
        d_act = dot(self.lhs[1, rows, :], w_out, NN)
        act, slope = gelu_both(pre)
        act = act.astype(BF16)
        d_pre = d_act * slope
        self.g_chan_in_bias[j] += fold(d_pre)
        d_pre = d_pre.astype(BF16)
        self.rhs[1 + slot, rows, :] = act
        self.rhs[0, rows, :] = d_pre
        if not late:
            self.total_out[rows, :] += dot(act, w_out, NT)
        self.total_din[rows, :] += dot(d_pre, w_in, NT)

    def weight_grad(self, matrix, slot):
        return dot(self.lhs[matrix], self.rhs[matrix * (1 + slot)], TN)

    def mixed_copies(self, pair, slot):
        return [
            pltpu.make_async_copy(self.mixed_slot.at[slot, k], self.mixed.at[pair * 2 + k], self.out_sem.at[slot, k, 0])
            for k in range(2)
        ]

    def finish_output(self, pair):
        sz, slot = self.sz, lax.rem(pair, 2)

        @pl.when(pair >= 2)
        def _():
            wait(self.mixed_copies(pair - 2, slot))

        both = self.both(pair)
        total = self.total_out[both, :]
        for late in range(2):
            total += dot(self.rhs[1 + late, both, :], self.weights_of(late, 1), NT)
        for k in range(2):
            layer = total[k * sz.padded : k * sz.padded + sz.padded] * self.kept(pair * 2 + k)
            self.mixed_slot[slot, k] = layer[: sz.patches].astype(BF16)
        start(self.mixed_copies(pair, slot))

    def finish_output_end(self):
        for pair in range(self.sz.pairs - 2, self.sz.pairs):
            wait(self.mixed_copies(pair, pair % 2))

    def token_backward(self, pair):
        sz, slot = self.sz, lax.rem(pair, 2)
        pad = sz.padded

        @pl.when(pair + 1 < sz.pairs)
        def _():
            start(self.back_copies(pair + 1, 1 - slot))

        @pl.when(pair >= 2)
        def _():
            for k in range(2):
                wait(self.result_copies(pair - 2, slot, k))

        self.next_images(pair)
        both = self.both(pair)
        d_in = self.total_din[both, :]
        hat = self.xhat2[both, :].astype(F32)
        self.g_gain2[...] += fold(d_in * hat)
        self.g_shift2[...] += fold(d_in)
        e = d_in * self.gain2[...]
        lane = lax.broadcasted_iota(jnp.int32, self.scale2.shape, 1)
        scale2 = jnp.sum(jnp.where(lane == pair, self.scale2[...], 0.0), axis=-1, keepdims=True)
        d_residual = self.lhs[1, both, :].astype(F32) + scale2 * (
            e - lane_mean(e) - hat * lane_mean(e * hat)
        )
        rounded = d_residual.astype(BF16).astype(F32)
        wait(self.back_copies(pair, slot))
        for k in range(2):
            i = pair * 2 + k
            part = slice(k * pad, (k + 1) * pad)
            d_token_out = rounded[part].astype(BF16)
            self.g_tok[1] += dot(self.act_slot[slot, k], d_token_out, NT)
            self.g_tok_out_bias[...] += jnp.sum(rounded[part], axis=-1, keepdims=True)
            d_pre = dot(self.tok_out[...], d_token_out, NN) * self.slope_slot[slot, k].astype(F32)
            d_pre = d_pre.astype(BF16)
            hat1, scale1 = standardize(self.image_of(pair, k))
            self.g_tok[0] += dot(d_pre, self.token_input(hat1), NT)
            d_token_in = dot(self.tok_in[...], d_pre, NN)
            self.g_gain1[...] += fold(d_token_in * hat1)
            self.g_shift1[...] += fold(d_token_in)
            f = d_token_in * self.gain1[...]
            result = d_residual[part] + scale1 * (f - lane_mean(f) - hat1 * lane_mean(f * hat1))
            self.gp_slot[slot, k] = result[: sz.patches].astype(BF16)
            start(self.result_copies(pair, slot, k))

    def token_backward_end(self):
        wait(self.load_copies(0, self.sz.pairs % 2))
        for pair in range(max(0, self.sz.pairs - 2), self.sz.pairs):
            for k in range(2):
                wait(self.result_copies(pair, pair % 2, k))


def layer_scratch(sz, weight_shape):
    images, patch, ch = sz.images, sz.patches, sz.channels
    return dict(
        x_slot=pltpu.VMEM((2, 2, patch, ch), BF16),
        lhs=pltpu.VMEM((2, sz.flat, ch), BF16), xhat2=pltpu.VMEM((sz.flat, ch), BF16),
        scale2=pltpu.VMEM((2 * sz.padded, 128), F32),
        total_out=pltpu.VMEM((sz.flat, ch), F32), total_din=pltpu.VMEM((sz.flat, ch), F32),
        act_slot=pltpu.VMEM((2, 2, sz.token_hidden, ch), BF16),
        slope_slot=pltpu.VMEM((2, 2, sz.token_hidden, ch), BF16),
        rhs=pltpu.VMEM((3, sz.flat, sz.width), BF16),
        w_slot=pltpu.VMEM((2, 2) + weight_shape + (sz.width,), BF16),
        mixed_slot=pltpu.VMEM((2, 2, patch, ch), BF16), gp_slot=pltpu.VMEM((2, 2, patch, ch), BF16),
        load_sem=pltpu.SemaphoreType.DMA((2, 2)), act_sem=pltpu.SemaphoreType.DMA((2, 2, 2)),
        w_sem=pltpu.SemaphoreType.DMA((2, 2)), out_sem=pltpu.SemaphoreType.DMA((2, 2, 2)),
    )


def layer_sums(sz):
    ch = sz.channels
    return dict(
        g_gain1=((8, ch), F32), g_shift1=((8, ch), F32), g_gain2=((8, ch), F32), g_shift2=((8, ch), F32),
        g_out_bias=((8, ch), F32), g_tok_out_bias=((sz.padded, 1), F32),
        g_tok=((2, sz.token_hidden, sz.padded), F32), g_chan_in_bias=((sz.blocks, 8, sz.width), F32),
    )


def layer_params(sz):
    ch, pad, th = sz.channels, sz.padded, sz.token_hidden
    return dict(
        gain1=((1, ch), F32), shift1=((1, ch), F32), gain2=((1, ch), F32), shift2=((1, ch), F32),
        out_bias=((1, ch), F32), tok_in_t=((th, pad), BF16), tok_in=((pad, th), BF16),
        tok_out_t=((pad, th), BF16), tok_out=((th, pad), BF16), chan_in_bias=((sz.blocks, 1, sz.width), F32),
    )


def layer_results(sz):
    return dict(
        mixed=((sz.images, sz.patches, sz.channels), BF16),
        grad_patches=((sz.images, sz.patches, sz.channels), BF16),
        kept_act=((sz.images, sz.token_hidden, sz.channels), BF16),
        kept_slope=((sz.images, sz.token_hidden, sz.channels), BF16),
    )


def call_kernel(kernel, inputs, outputs, scratch, vmem_mib, **params):
    names = list(inputs) + list(outputs) + list(scratch)

    def body(*refs):
        kernel(types.SimpleNamespace(**dict(zip(names, refs))))

    results = pl.pallas_call(
        body,
        out_shape=[jax.ShapeDtypeStruct(*of) for of, _ in outputs.values()],
        in_specs=[spec for _, spec in inputs.values()],
        out_specs=[spec for _, spec in outputs.values()],
        scratch_shapes=list(scratch.values()),
        compiler_params=pltpu.CompilerParams(vmem_limit_bytes=vmem_mib * 2**20, **params),
    )(*[array for array, _ in inputs.values()])
    return types.SimpleNamespace(**dict(zip(outputs, results)))


ANYWHERE = pl.BlockSpec(memory_space=pl.ANY)
VMEM = pl.BlockSpec(memory_space=pltpu.VMEM)
SMEM = pl.BlockSpec(memory_space=pltpu.SMEM)


def networked(sz, counts, patches, grad_out, **params):
    part = sz.channels // 16
    tok_part = sz.token_hidden // 16
    pack_rows = -(-(tok_part + 1) // 16) * 16
    blocks, width = sz.blocks, sz.width
    n_gather, n_reduce = blocks + 1, blocks

    def kernel(refs):
        place = Place()
        layer = Layer(sz, refs)
        gathered, pack_all = refs.gathered, refs.pack_all
        gather_sems = (refs.gather_send, refs.gather_recv)
        reduce_sems = (refs.reduce_send, refs.reduce_recv)
        vector_sems = (refs.vector_send, refs.vector_recv)
        own_out, tok_fin = refs.own_out, refs.tok_fin
        c = place.c
        chan_refs = [getattr(refs, "c%d" % k) for k in range(12)]
        tok_refs = [getattr(refs, "t%d" % k) for k in range(9)]

        def columns(j):
            return pl.ds(pl.multiple_of(j * width, width), width)

        def gather(j):
            cols = columns(j)

            def view(matrix, z, yx):
                return gathered.at[matrix, z, yx, :, cols]

            return Gather(place, refs.own_weight.at[:, cols], view, gather_sems, j * 7)

        def pack_view(matrix, z, yx):
            return pack_all.at[matrix, z, yx]

        pack = Gather(place, refs.pack_own, pack_view, gather_sems, blocks * 7)

        def reduce(j):
            return Reduce(place, chan_refs, own_out.at[c, :, columns(j)], reduce_sems, j * 7, lax.rem(j, 2))

        tok_reduce = SmallReduce(place, tok_refs, tok_fin.at[c], (refs.tok_send, refs.tok_recv))

        def own_load(source):
            return [pltpu.make_async_copy(source, refs.own_weight, refs.own_sem.at[2])]

        own_copies = [
            pltpu.make_async_copy(refs.own_weight, gathered.at[c, place.z, place.yx], refs.own_sem.at[0]),
            pltpu.make_async_copy(refs.pack_own, pack_all.at[c, place.z, place.yx], refs.own_sem.at[1]),
        ]

        def weight_loads(j, slot):
            return [
                pltpu.make_async_copy(
                    gathered.at[m, :, :, :, columns(j)], layer.w_slot.at[slot, m], layer.w_sem.at[slot, m]
                )
                for m in range(2)
            ]

        @pl.when(c == 0)
        def _():
            start(own_load(refs.p_w_chan_in))

        @pl.when(c == 1)
        def _():
            start(own_load(refs.p_w_chan_out))

        layer.begin()
        make_pack(sz, c, refs)
        wait(own_load(refs.p_w_chan_in))
        start(own_copies)
        place.greet()
        start(pack.along_z)
        start(gather(0).along_z)
        layer.clear()
        lax.fori_loop(0, sz.pairs, layer.mask_pair, 0)
        wait(own_copies)
        pack.to_xy()
        lax.fori_loop(0, sz.pairs // 2, layer.norm_pair, 0)
        gather(0).to_a()
        start(gather(1).along_z)
        lax.fori_loop(sz.pairs // 2, sz.pairs, layer.norm_pair, 0)
        pack.xy_to_sibling()
        wait(pack.swap)
        unpack(sz, layer, pack_all, tok_part)
        gather(0).to_b()
        gather(1).to_a()
        start(gather(2).along_z)

        def forward_step(pair, carry):
            layer.token_forward(pair)

            @pl.when(pair == 3)
            def _():
                gather(0).to_sibling()
                gather(1).to_b()
                gather(2).to_a()
                start(gather(3).along_z)

            @pl.when(pair == 5)
            def _():
                wait(gather(0).swap)
                start(weight_loads(0, 0))

            return carry

        lax.fori_loop(0, sz.pairs, forward_step, 0)
        layer.token_forward_end()

        start(layer.back_copies(0, 0))

        def block_step(late, j, carry):
            slot = lax.rem(j, 2)
            wait(weight_loads(j, slot))

            def chunk(r, carry):
                layer.row_chunk(j, slot, r, late)

                @pl.when(r == 0)
                def _():
                    @pl.when(j >= 3)
                    def _():
                        reduce(j - 3).to_owner()

                    @pl.when(j >= 1)
                    def _():
                        reduce(j - 1).to_b()

                @pl.when(r == 1)
                def _():
                    @pl.when(j + 1 < blocks)
                    def _():
                        gather(j + 1).to_sibling()

                    @pl.when(j + 2 < blocks)
                    def _():
                        gather(j + 2).to_b()

                    @pl.when(j + 3 < blocks)
                    def _():
                        gather(j + 3).to_a()

                    @pl.when(j + 4 < blocks)
                    def _():
                        start(gather(j + 4).along_z)

                @pl.when(r == 2)
                def _():
                    @pl.when(j >= 2)
                    def _():
                        reduce(j - 2).to_z()

                return carry

            lax.fori_loop(0, sz.chunks, chunk, 0)
            mine, csend = chan_refs[0], chan_refs[1]
            csend[...] = layer.weight_grad(1 - c, slot).astype(BF16).reshape(csend.shape)
            start(reduce(j).swap)

            @pl.when(j + 1 < blocks)
            def _():
                wait(gather(j + 1).swap)
                start(weight_loads(j + 1, 1 - slot))

            mine[...] = layer.weight_grad(c, slot).astype(BF16).reshape(mine.shape)

            @pl.when(j >= 1)
            def _():
                reduce(j - 1).to_a()

            return carry

        lax.fori_loop(0, blocks - 2, functools.partial(block_step, False), 0)
        lax.fori_loop(blocks - 2, blocks, functools.partial(block_step, True), 0)

        def backward_step(pair, carry):
            layer.token_backward(pair)

            @pl.when(pair == 0)
            def _():
                reduce(blocks - 3).to_owner()
                reduce(blocks - 1).to_b()

            @pl.when(pair == 1)
            def _():
                reduce(blocks - 2).to_z()

            @pl.when(pair == 3)
            def _():
                reduce(blocks - 2).to_owner()
                reduce(blocks - 1).to_a()

            @pl.when(pair == 5)
            def _():
                reduce(blocks - 1).to_z()

            return carry

        lax.fori_loop(0, sz.pairs, backward_step, 0)

        mine, csend = tok_refs[0], tok_refs[1]

        def packed(matrix):
            value = layer.g_tok[matrix].reshape(16, tok_part, sz.padded)
            return value

        filler = jnp.zeros((16, pack_rows - tok_part, sz.padded), F32)
        for ref, matrix in ((csend, 1 - c), (mine, c)):
            value = jnp.concatenate([packed(matrix), filler], axis=1).astype(ref.dtype)
            ref[:, :, :, 0 : sz.padded] = value.reshape(4, 4, pack_rows, sz.padded)
            ref[:, :, :, sz.padded :] = jnp.zeros((4, 4, pack_rows, sz.lanes - sz.padded), ref.dtype)
            if ref is csend:
                start(tok_reduce.swap)
        vec, vec_in, vec_xy, vec_z = refs.vec, refs.vec_in, refs.vec_xy, refs.vec_z
        vec[...] = jnp.zeros_like(vec)
        for k, ref in enumerate((layer.g_gain1, layer.g_shift1, layer.g_gain2, layer.g_shift2, layer.g_out_bias)):
            vec[k : k + 1, :] = jnp.sum(ref[...], axis=0, keepdims=True)
        column = jnp.broadcast_to(layer.g_tok_out_bias[...], (sz.padded, 128))
        vec[5:6, 0 : sz.padded] = jnp.transpose(column)[0:1]
        flat = [jnp.sum(layer.g_chan_in_bias[j], axis=0, keepdims=True) for j in range(blocks)]
        flat = jnp.concatenate(flat, axis=1)
        for k in range(sz.hidden // sz.channels):
            vec[6 + k : 7 + k, :] = flat[:, k * sz.channels : (k + 1) * sz.channels]

        vector_swap = [remote(vec, vec_in, vector_sems, 0, place.sibling)]
        vector_xy = [remote(vec, vec_xy.at[place.yx], vector_sems, 1 + k, place.peers_xy[k]) for k in range(3)]
        vector_z = [remote(vec, vec_z.at[place.z], vector_sems, 3 + k, place.peer_z[k]) for k in (1, 2, 3)]
        def output(pair, carry):
            layer.finish_output(pair)
            return carry

        start(vector_swap)
        reduce(blocks - 1).to_owner()
        lax.fori_loop(0, 1, output, 0)
        tok_reduce.to_xy()
        wait(vector_swap)
        vec[...] += vec_in[...]
        start(vector_xy)
        vec_xy[place.yx] = vec[...]
        lax.fori_loop(1, 4, output, 0)
        tok_reduce.to_z()
        wait(vector_xy)
        vec[...] = (vec_xy[0] + vec_xy[1]) + (vec_xy[2] + vec_xy[3])
        start(vector_z)
        vec_z[place.z] = vec[...]
        lax.fori_loop(4, sz.pairs, output, 0)
        layer.token_backward_end()
        layer.finish_output_end()
        tok_reduce.to_owner()
        wait(vector_z)
        refs.vec_out[...] = (vec_z[0] + vec_z[1]) + (vec_z[2] + vec_z[3])

        def finish(j, carry):
            wait(reduce(j).finish)
            return carry

        lax.fori_loop(0, blocks, finish, 0)
        wait(tok_reduce.finish)

    inputs = dict(counts=(counts, SMEM), patches=(patches, ANYWHERE), grad_out=(grad_out, ANYWHERE))
    inputs.update({"p_" + name: (of, ANYWHERE if name[:6] == "w_chan" else VMEM) for name, of in params.items()})
    outputs = {name: (of, ANYWHERE) for name, of in layer_results(sz).items()}
    outputs.update(
        gathered=(((2, 4, 4, part, sz.hidden), BF16), ANYWHERE), own_out=(((2, part, sz.hidden), F32), VMEM),
        tok_fin=(((2, pack_rows, sz.lanes), F32), VMEM), vec_out=(((16, sz.channels), F32), VMEM),
    )
    scratch = layer_scratch(sz, (4, 4, part))
    for group in (layer_sums(sz), layer_params(sz)):
        scratch.update({name: pltpu.VMEM(*of) for name, of in group.items()})
    scratch.update({"c%d" % k: of for k, of in enumerate(reduce_scratch(part, width, 2))})
    scratch.update({"t%d" % k: of for k, of in enumerate(small_reduce_scratch(pack_rows, sz.lanes))})
    dma = pltpu.SemaphoreType.DMA
    scratch.update(
        pack_all=pltpu.VMEM((2, 4, 4, pack_rows, sz.lanes), BF16), pack_own=pltpu.VMEM((pack_rows, sz.lanes), BF16),
        pack_tmp=pltpu.VMEM((pack_rows, sz.lanes), F32), own_weight=pltpu.VMEM((part, sz.hidden), BF16),
        tok_out_bias=pltpu.VMEM((sz.padded, 1), F32),
        vec=pltpu.VMEM((16, sz.channels), F32), vec_in=pltpu.VMEM((16, sz.channels), F32),
        vec_xy=pltpu.VMEM((4, 16, sz.channels), F32), vec_z=pltpu.VMEM((4, 16, sz.channels), F32), own_sem=dma((3,)),
        gather_send=dma((n_gather * 7,)), gather_recv=dma((n_gather * 7,)),
        reduce_send=dma((n_reduce * 7,)), reduce_recv=dma((n_reduce * 7,)),
        tok_send=dma((8,)), tok_recv=dma((8,)), vector_send=dma((7,)), vector_recv=dma((7,)),
    )
    return call_kernel(kernel, inputs, outputs, scratch, 62, collective_id=0, has_side_effects=True)


def make_pack(sz, c, refs):
    tmp = refs.pack_tmp
    tok_in, tok_out = refs.p_w_token_in, refs.p_w_token_out
    tok_part = tok_out.shape[0]

    def row(*sources):
        values = [source[...].astype(F32)[None, :] for source in sources]
        rest = sz.lanes - sum(value.shape[1] for value in values)
        return jnp.concatenate(values + [jnp.zeros((1, rest), F32)], axis=1)

    tmp[...] = jnp.zeros_like(tmp)
    tmp[0:tok_part, 0 : sz.patches] = jnp.where(c == 0, tok_in[...].astype(F32), tok_out[...].astype(F32))
    first = row(refs.p_ln1_gain, refs.p_ln1_bias, refs.p_ln2_gain, refs.p_ln2_bias, refs.p_b_chan_out)
    tmp[tok_part : tok_part + 1, :] = jnp.where(c == 0, first, row(refs.p_b_chan_in, refs.p_b_token_in))
    refs.pack_own[...] = tmp[...].astype(BF16)
    bias = jnp.broadcast_to(row(refs.p_b_token_out), (8, sz.lanes))
    refs.tok_out_bias[...] = jnp.transpose(bias)[0 : sz.padded, 0:1]


def spread(rows, length, lanes, first_lane, columns):
    at = lax.broadcasted_iota(jnp.int32, (1, columns[1] - columns[0]), 1) + columns[0]
    device = jnp.zeros_like(at)
    for k in range(1, 16):
        device += jnp.where(at >= k * length, 1, 0)
    source = at - device * length + first_lane
    lane = lax.broadcasted_iota(jnp.int32, (lanes, source.shape[1]), 0)
    chosen = jnp.where(lane == source, 1.0, 0.0).astype(BF16)
    value = dot(rows, chosen, NN)
    owner = lax.broadcasted_iota(jnp.int32, value.shape, 0)
    return jnp.sum(jnp.where(owner == device, value, 0.0), axis=0, keepdims=True)


def unpack(sz, layer, pack_all, tok_part):
    pad, lanes, ch = sz.padded, sz.lanes, sz.channels
    rows = pack_all.shape[3]
    both = [pack_all[m].reshape(16, rows, lanes).astype(F32) for m in range(2)]
    first, second = (value[:, :tok_part].reshape(sz.token_hidden, lanes) for value in both)
    vectors, biases = (value[:, tok_part].astype(BF16) for value in both)
    part = ch // 16
    for v, ref in enumerate((layer.gain1, layer.shift1, layer.gain2, layer.shift2, layer.out_bias)):
        ref[...] = spread(vectors, part, lanes, v * part, (0, ch))
    for j in range(sz.blocks):
        layer.chan_in_bias[j] = spread(biases, sz.hidden // 16, lanes, 0, (j * sz.width, (j + 1) * sz.width))
    bias = spread(biases, tok_part, lanes, sz.hidden // 16, (0, sz.token_hidden))
    bias = jnp.transpose(jnp.broadcast_to(bias, (8, sz.token_hidden)))[:, 0:1]
    column = lax.broadcasted_iota(jnp.int32, first.shape, 1)
    layer.tok_in_t[...] = jnp.where(column == sz.patches, bias, first)[:, :pad].astype(BF16)
    layer.tok_out[...] = second[:, :pad].astype(BF16)
    layer.tok_in[...] = jnp.transpose(first)[:pad].astype(BF16)
    layer.tok_out_t[...] = jnp.transpose(second)[:pad].astype(BF16)


def hand_out(sz, raw, tok_part, hidden_part):
    part = raw.own_out.shape[1]
    images, patch, ch = sz.images, sz.patches, sz.channels

    def kernel(refs):
        load_sem, store_sem, own_sem = refs.load_sem, refs.store_sem, refs.own_sem

        def loads(i):
            return [
                pltpu.make_async_copy(refs.raw_mixed.at[i], refs.tmp_mixed.at[i], load_sem.at[0, i]),
                pltpu.make_async_copy(refs.raw_grad.at[i], refs.tmp_grad.at[i], load_sem.at[1, i]),
            ]

        def stores(i):
            return [
                pltpu.make_async_copy(refs.tmp_mixed.at[i], refs.mixed.at[i], store_sem.at[0, i]),
                pltpu.make_async_copy(refs.tmp_wide.at[i], refs.grad_patches.at[i], store_sem.at[1, i]),
            ]

        def load(i, carry):
            start(loads(i))
            return carry

        def store(i, carry):
            wait(loads(i))
            refs.tmp_wide[i] = refs.tmp_grad[i].astype(F32)
            start(stores(i))
            return carry

        def finish(i, carry):
            wait(stores(i))
            return carry

        own_loads = [pltpu.make_async_copy(refs.own, refs.tmp_own, own_sem.at[0])]
        own_stores = [
            pltpu.make_async_copy(refs.tmp_own.at[m], target, own_sem.at[1 + m])
            for m, target in enumerate((refs.g_chan_in, refs.g_chan_out))
        ]
        lax.fori_loop(0, images, load, 0)
        start(own_loads)
        lax.fori_loop(0, images, store, 0)
        wait(own_loads)
        start(own_stores)
        me = lax.axis_index("dp")
        vec, tok = refs.vec, refs.tok
        across = pltpu.roll(vec[...], ch - me * part, axis=1)
        for k, ref in enumerate((refs.g_gain1, refs.g_shift1, refs.g_gain2, refs.g_shift2, refs.g_out_bias)):
            ref[...] = across[k, 0:part]
        refs.g_tok_out_bias[...] = vec[5, 0:patch]
        per_row = ch // hidden_part
        row = vec[pl.ds(6 + me // per_row, 1), :]
        refs.g_chan_in_bias[...] = pltpu.roll(row, ch - lax.rem(me, per_row) * hidden_part, axis=1)[0, 0:hidden_part]
        refs.g_tok_out[...] = tok[1, 0:tok_part, 0:patch]
        refs.g_tok_in[...] = tok[0, 0:tok_part, 0:patch]
        refs.g_tok_in_bias[...] = jnp.transpose(tok[0])[patch, 0:tok_part]
        wait(own_stores)
        lax.fori_loop(0, images, finish, 0)

    inputs = dict(
        raw_mixed=(raw.mixed, ANYWHERE), raw_grad=(raw.grad_patches, ANYWHERE), own=(raw.own_out, ANYWHERE),
        tok=(raw.tok_fin, VMEM), vec=(raw.vec_out, VMEM),
    )
    vector, big = ((part,), F32), ((part, sz.hidden), F32)
    outputs = dict(
        mixed=(((images, patch, ch), BF16), ANYWHERE), grad_patches=(((images, patch, ch), F32), ANYWHERE),
        g_gain1=(vector, VMEM), g_shift1=(vector, VMEM), g_tok_in=(((tok_part, patch), F32), VMEM),
        g_tok_in_bias=(((tok_part,), F32), VMEM), g_tok_out=(((tok_part, patch), F32), VMEM),
        g_tok_out_bias=(((patch,), F32), VMEM), g_gain2=(vector, VMEM), g_shift2=(vector, VMEM),
        g_chan_in=(big, ANYWHERE), g_chan_in_bias=(((hidden_part,), F32), VMEM), g_chan_out=(big, ANYWHERE),
        g_out_bias=(vector, VMEM),
    )
    dma = pltpu.SemaphoreType.DMA
    scratch = dict(
        tmp_mixed=pltpu.VMEM((images, patch, ch), BF16), tmp_grad=pltpu.VMEM((images, patch, ch), BF16),
        tmp_wide=pltpu.VMEM((images, patch, ch), F32), tmp_own=pltpu.VMEM((2, part, sz.hidden), F32),
        load_sem=dma((2, images)), store_sem=dma((2, images)), own_sem=dma((3,)),
    )
    results = call_kernel(kernel, inputs, outputs, scratch, 62)
    results.g_tok_in, results.g_chan_out = results.g_tok_in.T, results.g_chan_out.T
    return tuple(vars(results).values())


def local(sz, counts, patches, grad_out, weights, tok_out_bias, params):
    def kernel(refs):
        layer = Layer(sz, refs)
        gw_slot, gw_sem = refs.gw_slot, refs.gw_sem

        def columns(j):
            return pl.ds(pl.multiple_of(j * sz.width, sz.width), sz.width)

        def weight_loads(j, slot):
            return [
                pltpu.make_async_copy(refs.weights.at[m, :, columns(j)], layer.w_slot.at[slot, m], layer.w_sem.at[slot, m])
                for m in range(2)
            ]

        def grad_stores(j, m):
            return [pltpu.make_async_copy(gw_slot.at[m], refs.g_weights.at[m, :, columns(j)], gw_sem.at[m])]

        layer.begin()
        start(weight_loads(0, 0))
        layer.clear()
        lax.fori_loop(0, sz.pairs, layer.mask_pair, 0)
        lax.fori_loop(0, sz.pairs, layer.norm_pair, 0)

        def forward_step(pair, carry):
            layer.token_forward(pair)
            return carry

        lax.fori_loop(0, sz.pairs, forward_step, 0)
        layer.token_forward_end()

        start(layer.back_copies(0, 0))

        def block_step(late, j, carry):
            slot = lax.rem(j, 2)
            wait(weight_loads(j, slot))

            @pl.when(j + 1 < sz.blocks)
            def _():
                start(weight_loads(j + 1, 1 - slot))

            def chunk(r, carry):
                layer.row_chunk(j, slot, r, late)
                return carry

            lax.fori_loop(0, sz.chunks, chunk, 0)
            for m in range(2):

                @pl.when(j >= 1)
                def _():
                    wait(grad_stores(j - 1, m))

                gw_slot[m] = layer.weight_grad(m, slot)
                start(grad_stores(j, m))
            return carry

        lax.fori_loop(0, sz.blocks - 2, functools.partial(block_step, False), 0)
        lax.fori_loop(sz.blocks - 2, sz.blocks, functools.partial(block_step, True), 0)
        for m in range(2):
            wait(grad_stores(sz.blocks - 1, m))

        def backward_step(pair, carry):
            layer.token_backward(pair)
            return carry

        lax.fori_loop(0, sz.pairs, backward_step, 0)
        layer.token_backward_end()

        def output(pair, carry):
            layer.finish_output(pair)
            return carry

        lax.fori_loop(0, sz.pairs, output, 0)
        layer.finish_output_end()

    inputs = dict(
        counts=(counts, SMEM), patches=(patches, ANYWHERE), grad_out=(grad_out, ANYWHERE), weights=(weights, ANYWHERE),
        tok_out_bias=(tok_out_bias, VMEM),
    )
    inputs.update({name: (params[name], VMEM) for name in layer_params(sz)})
    outputs = {name: (of, ANYWHERE) for name, of in layer_results(sz).items()}
    outputs.update(g_weights=(((2, sz.channels, sz.hidden), F32), ANYWHERE))
    outputs.update({name: (of, VMEM) for name, of in layer_sums(sz).items()})
    scratch = layer_scratch(sz, (sz.channels,))
    scratch.update(gw_slot=pltpu.VMEM((2, sz.channels, sz.width), F32), gw_sem=pltpu.SemaphoreType.DMA((2,)))
    return call_kernel(kernel, inputs, outputs, scratch, 62)


def on_device(
    patches, image_counts, grad_out,
    ln1_gain, ln1_bias, w_token_in, b_token_in, w_token_out, b_token_out,
    ln2_gain, ln2_bias, w_chan_in, b_chan_in, w_chan_out, b_chan_out,
):
    images, patch, ch = patches.shape
    token_part, hidden_part, part = b_token_in.shape[0], b_chan_in.shape[0], ln1_gain.shape[0]
    n_dp = lax.axis_size("dp")
    hidden = w_chan_in.shape[1]
    sz = Sizes(images, patch, ch, token_part * n_dp, hidden, 512, images * (-(-patch // 8) * 8) // 3)
    pad = sz.padded
    vectors = (ln1_gain, ln1_bias, ln2_gain, ln2_bias, b_chan_out)

    def own(vector, length):
        return lax.dynamic_slice_in_dim(vector, lax.axis_index("dp") * length, length)

    if n_dp == 16 and sz.pairs == 6 and part % 16 == 0 and token_part % 8 == 0 and part % token_part == 0:
        res = networked(
            sz, image_counts, patches, grad_out, ln1_gain=ln1_gain, ln1_bias=ln1_bias, w_token_in=w_token_in.T,
            b_token_in=b_token_in, w_token_out=w_token_out, b_token_out=b_token_out, ln2_gain=ln2_gain,
            ln2_bias=ln2_bias, w_chan_in=w_chan_in, b_chan_in=b_chan_in, w_chan_out=w_chan_out.T,
            b_chan_out=b_chan_out,
        )
        return hand_out(sz, res, token_part, hidden_part)
    else:
        tok_out_bias = jnp.pad(b_token_out.astype(F32), (0, pad - patch))[:, None]
        weights = lax.all_gather(jnp.stack([w_chan_in, w_chan_out.T]), "dp", axis=1, tiled=True)
        tokens = lax.all_gather(jnp.stack([w_token_in.T, w_token_out]), "dp", axis=1, tiled=True)
        tokens = jnp.pad(tokens, ((0, 0), (0, 0), (0, pad - patch)))
        every = lax.all_gather(jnp.concatenate(vectors + (b_token_in, b_chan_in)), "dp", axis=0)
        whole = [every[:, k * part : (k + 1) * part].reshape(1, ch).astype(F32) for k in range(5)]
        tok_bias = every[:, 5 * part : 5 * part + token_part].reshape(-1)
        gain1, shift1, gain2, shift2, out_bias = whole
        params = dict(
            gain1=gain1, shift1=shift1, gain2=gain2, shift2=shift2, out_bias=out_bias,
            tok_in_t=tokens[0].at[:, patch].set(tok_bias), tok_in=tokens[0].T,
            tok_out_t=tokens[1].T, tok_out=tokens[1],
            chan_in_bias=every[:, 5 * part + token_part :].reshape(sz.blocks, 1, sz.width).astype(F32),
        )
        res = local(sz, image_counts, patches, grad_out, weights, tok_out_bias, params)
        g_weights = lax.psum_scatter(res.g_weights.astype(BF16), "dp", scatter_dimension=1, tiled=True)
        g_weights = lax.psum(g_weights, "outer").astype(F32)
        g_tokens = lax.psum(lax.psum_scatter(res.g_tok, "dp", scatter_dimension=1, tiled=True), "outer")
        sums = [jnp.sum(v, axis=0) for v in (res.g_gain1, res.g_shift1, res.g_gain2, res.g_shift2, res.g_out_bias)]
        sums += [jnp.sum(res.g_chan_in_bias, axis=1).reshape(-1), res.g_tok_out_bias[:patch, 0]]
        sums = lax.psum(tuple(sums), ("dp", "outer"))
        g_vec = [own(vector, part) for vector in sums[:5]]
        g_chan_bias, g_tok_out_bias = own(sums[5], hidden_part), sums[6]

    return (
        res.mixed, res.grad_patches.astype(F32),
        g_vec[0], g_vec[1], g_tokens[0, :, :patch].T, g_tokens[0, :, patch], g_tokens[1, :, :patch], g_tok_out_bias,
        g_vec[2], g_vec[3], g_weights[0], g_chan_bias, g_weights[1].T, g_vec[4],
    )


def solution(mesh):
    slots = P(("dp", "outer"), None, None)
    return jax.shard_map(
        on_device,
        mesh=mesh,
        in_specs=(
            slots, P(("dp", "outer")), slots, P("dp"), P("dp"), P(None, "dp"), P("dp"), P("dp", None), P(),
            P("dp"), P("dp"), P("dp", None), P("dp"), P(None, "dp"), P("dp"),
        ),
        out_specs=(
            slots, slots, P("dp"), P("dp"), P(None, "dp"), P("dp"), P("dp", None), P(),
            P("dp"), P("dp"), P("dp", None), P("dp"), P(None, "dp"), P("dp"),
        ),
        check_vma=False,
    )
```

time: 215 us -> 165 us (0.77)
  local copies, waits for them, and re-layouts: 25.7 us -> 0 us
  Pallas kernels: 183 us -> 163 us
  other arithmetic: 5.05 us -> 0 us
    pallas_call x1 -> x2, Pallas kernels: 183 us -> 163 us  [call_kernel(): pl.pallas_call(body, out_shape=[jax.ShapeDtypeStruct(*of) for of, _ in ou...]
    unnamed x4 -> x0, local copies, waits for them, and re-layouts: 8.59 us -> none
    slice x4 -> x0, local copies, waits for them, and re-layouts: 4.36 us -> none  [the longest x1 1.4 us: on_device(): g_tokens[0, :, patch]]
    reshape x11 -> x0, local copies, waits for them, and re-layouts: 4.2 us -> none  [the longest x10 4.19 us: make_pack(): cols = [vector.reshape(runs, tok_part).T for vector in vectors]]
    select_n x4 -> x0, other arithmetic: 3.25 us -> none  [the longest x1 1.8 us: on_device(): own_weight = jnp.where(c == 0, w_chan_in, w_chan_out.T)]
    dynamic_slice x4 -> x0, local copies, waits for them, and re-layouts: 2.39 us -> none  [own(): lax.dynamic_slice_in_dim(vector, lax.axis_index('dp') * length, length)]
    transpose x1 -> x0, local copies, waits for them, and re-layouts: 2.33 us -> none  [on_device(): g_weights[1]]
where the time goes in v3:
time: 165 us
  Pallas kernels  163 us (99%)
    pallas_call x2, Pallas kernels, call_kernel(): pl.pallas_call(body, out_shape=[jax.ShapeDtypeStruct(*of) for of, _ in ou...  163 us

profile of v3, /device:TPU:0, one launch (start us, length us, event | category | flops | bytes accessed | tf_op | source)
XLA Modules:
  0.0 164.9 jit_solution(13852720813157342010)
XLA Ops:
  1.3 153.5 %shard_map.254 = (bf16[12,196,768]{2,1,0:T(8,128)(2,1)}, bf16[12,196,768]{2,1,0:T(8,128)(2,1)}, bf16[12,384,768]{2,1,0:T(8,128)(2,1)}, bf16[12,384,768]{2,1,0:T(...) custom-call(s32[1]{0:T(128)S(6)} %copy.29.refs_0_, ...), custom_call_target="tpu_custom_call" | custom-call | tf_op jit(solution)/shard_map/pallas_call | solution.py:607
  154.8 10.0 %shard_map.255 = (bf16[12,196,768]{2,1,0:T(8,128)(2,1)}, f32[12,196,768]{2,1,0:T(8,128)}, f32[48]{0:T(128)}, f32[48]{0:T(128)}, f32[24,196]{1,0:T(8,128)}, /*ind...) custom-call(bf16[12,196,768]{2,1,0:T(8,128)(2,1)} %get-tuple-element, ...), custom_call_target="tpu_custom_call" | custom-call | tf_op jit(solution)/shard_map/pallas_call | solution.py:607

commit v4 on v3

--- a/solution.py
+++ b/solution.py
@@ -95,10 +95,11 @@
 
     def greet(self):
         barrier = pltpu.get_barrier_semaphore()
-        peers = [self.sibling] + self.peers_xy + self.peer_z[1:]
-        for peer in peers:
+        for peer in [self.sibling] + self.peers_xy + self.peer_z[1:]:
             pl.semaphore_signal(barrier, inc=1, device_id=peer, device_id_type=MESH)
-        pl.semaphore_wait(barrier, len(peers))
+
+    def meet(self):
+        pl.semaphore_wait(pltpu.get_barrier_semaphore(), 7)
 
 
 def remote(source, target, sems, index, peer):
@@ -676,6 +677,8 @@
                 for m in range(2)
             ]
 
+        place.greet()
+
         @pl.when(c == 0)
         def _():
             start(own_load(refs.p_w_chan_in))
@@ -686,10 +689,10 @@
 
         layer.begin()
         make_pack(sz, c, refs)
+        place.meet()
+        start(pack.along_z)
         wait(own_load(refs.p_w_chan_in))
         start(own_copies)
-        place.greet()
-        start(pack.along_z)
         start(gather(0).along_z)
         layer.clear()
         lax.fori_loop(0, sz.pairs, layer.mask_pair, 0)
@@ -737,9 +740,9 @@
 
                 @pl.when(r == 0)
                 def _():
-                    @pl.when(j >= 3)
+                    @pl.when(j >= 2)
                     def _():
-                        reduce(j - 3).to_owner()
+                        reduce(j - 2).to_a()
 
                     @pl.when(j >= 1)
                     def _():
@@ -765,9 +768,9 @@
 
                 @pl.when(r == 2)
                 def _():
-                    @pl.when(j >= 2)
+                    @pl.when(j >= 3)
                     def _():
-                        reduce(j - 2).to_z()
+                        reduce(j - 3).to_owner()
 
                 return carry
 
@@ -783,9 +786,9 @@
 
             mine[...] = layer.weight_grad(c, slot).astype(BF16).reshape(mine.shape)
 
-            @pl.when(j >= 1)
+            @pl.when(j >= 2)
             def _():
-                reduce(j - 1).to_a()
+                reduce(j - 2).to_z()
 
             return carry
 
@@ -797,21 +800,21 @@
 
             @pl.when(pair == 0)
             def _():
-                reduce(blocks - 3).to_owner()
+                reduce(blocks - 2).to_a()
                 reduce(blocks - 1).to_b()
 
             @pl.when(pair == 1)
             def _():
+                reduce(blocks - 3).to_owner()
+
+            @pl.when(pair == 2)
+            def _():
                 reduce(blocks - 2).to_z()
 
-            @pl.when(pair == 3)
+            @pl.when(pair == 4)
             def _():
                 reduce(blocks - 2).to_owner()
                 reduce(blocks - 1).to_a()
-
-            @pl.when(pair == 5)
-            def _():
-                reduce(blocks - 1).to_z()
 
             return carry
 
@@ -849,8 +852,8 @@
             return carry
 
         start(vector_swap)
-        reduce(blocks - 1).to_owner()
         lax.fori_loop(0, 1, output, 0)
+        reduce(blocks - 1).to_z()
         tok_reduce.to_xy()
         wait(vector_swap)
         vec[...] += vec_in[...]
@@ -865,6 +868,7 @@
         lax.fori_loop(4, sz.pairs, output, 0)
         layer.token_backward_end()
         layer.finish_output_end()
+        reduce(blocks - 1).to_owner()
         tok_reduce.to_owner()
         wait(vector_z)
         refs.vec_out[...] = (vec_z[0] + vec_z[1]) + (vec_z[2] + vec_z[3])

time: 165 us -> 162 us (0.982)
  Pallas kernels: 163 us -> 160 us
    pallas_call x2, Pallas kernels: 163 us -> 160 us  [call_kernel(): pl.pallas_call(body, out_shape=[jax.ShapeDtypeStruct(*of) for of, _ in ou...]
where the time goes in v4:
time: 162 us; the launch traced here: 161 us
  Pallas kernels  160 us (99%)
    pallas_call x2, Pallas kernels, call_kernel(): pl.pallas_call(body, out_shape=[jax.ShapeDtypeStruct(*of) for of, _ in ou...  160 us

profile of v4, /device:TPU:0, one launch (start us, length us, event | category | flops | bytes accessed | tf_op | source)
XLA Modules:
  0.0 161.2 jit_solution(1688754644667506739)
XLA Ops:
  1.3 149.7 %shard_map.254 = (bf16[12,196,768]{2,1,0:T(8,128)(2,1)}, bf16[12,196,768]{2,1,0:T(8,128)(2,1)}, bf16[12,384,768]{2,1,0:T(8,128)(2,1)}, bf16[12,384,768]{2,1,0:T(...) custom-call(s32[1]{0:T(128)S(6)} %copy.29.refs_0_, ...), custom_call_target="tpu_custom_call" | custom-call | tf_op jit(solution)/shard_map/pallas_call | solution.py:608
  151.1 10.0 %shard_map.255 = (bf16[12,196,768]{2,1,0:T(8,128)(2,1)}, f32[12,196,768]{2,1,0:T(8,128)}, f32[48]{0:T(128)}, f32[48]{0:T(128)}, f32[24,196]{1,0:T(8,128)}, /*ind...) custom-call(bf16[12,196,768]{2,1,0:T(8,128)(2,1)} %get-tuple-element, ...), custom_call_target="tpu_custom_call" | custom-call | tf_op jit(solution)/shard_map/pallas_call | solution.py:608
